TPU v7x, 32 devices: a whole 2x2x4 slice. The times are simulated.
32 devices in a mesh: dp: 8 (over z, x), tensor: 4 (over y, core).
Axes of the slice: x: 2, y: 2, z: 4, core: 2. Of those that a mesh axis runs over, the one named last changes fastest.
Arguments:
- tokens: bfloat16 [16384, 1152], P(('dp', 'tensor')), may hold values from -6 to 6
- gain_one: float32 [1152], replicated, may hold values from 0.5 to 1.5
- shift_one: float32 [1152], replicated, may hold values from -2 to 2
- w_query: float32 [1152, 1152], P('dp', 'tensor'), may hold values from -0.25 to 0.25
- b_query: float32 [1152], replicated, may hold values from -2 to 2
- w_key: float32 [1152, 1152], P('dp', 'tensor'), may hold values from -0.25 to 0.25
- w_value: float32 [1152, 1152], P('dp', 'tensor'), may hold values from -0.1875 to 0.1875
- b_value: float32 [1152], replicated, may hold values from -2 to 2
- w_out: float32 [1152, 1152], P('tensor', 'dp'), may hold values from -0.75 to 0.75
- b_out: float32 [1152], replicated, may hold values from -2 to 2
- gain_two: float32 [1152], replicated, may hold values from 0.5 to 1.5
- shift_two: float32 [1152], replicated, may hold values from -2 to 2
- w_up: float32 [1152, 4304], P('dp', 'tensor'), may hold values from -0.1875 to 0.1875
- b_up: float32 [4304], replicated, may hold values from -2 to 2
- w_down: float32 [4304, 1152], P('tensor', 'dp'), may hold values from -0.09375 to 0.09375
- b_down: float32 [1152], replicated, may hold values from -2 to 2
- cotangent: bfloat16 [16384, 1152], P(('dp', 'tensor')), may hold values from -6 to 6
Outputs:
- output: bfloat16 [16384, 1152], P(('dp', 'tensor'))
- grad_tokens: bfloat16 [16384, 1152], P(('dp', 'tensor'))
- grad_gain_one: float32 [1152], replicated
- grad_shift_one: float32 [1152], replicated
- grad_w_query: float32 [1152, 1152], P('dp', 'tensor')
- grad_b_query: float32 [1152], replicated
- grad_w_key: float32 [1152, 1152], P('dp', 'tensor')
- grad_w_value: float32 [1152, 1152], P('dp', 'tensor')
- grad_b_value: float32 [1152], replicated
- grad_w_out: float32 [1152, 1152], P('tensor', 'dp')
- grad_b_out: float32 [1152], replicated
- grad_gain_two: float32 [1152], replicated
- grad_shift_two: float32 [1152], replicated
- grad_w_up: float32 [1152, 4304], P('dp', 'tensor')
- grad_b_up: float32 [4304], replicated
- grad_w_down: float32 [4304, 1152], P('tensor', 'dp')
- grad_b_down: float32 [1152], replicated
All inputs are finite; a program needn't handle non-finite values.
Results may differ from a plain program's by a relative error of at most 0.02.
Values may be sent and summed in bfloat16 or wider, within the bound.
No kernel may reach another device: no remote copies, remote signals or barrier semaphores. Data moves between devices by JAX's collectives and lax.ppermute only.
A program may use at most 192 MiB of HBM per device.

v0:
```python
import functools
import math

import jax
import jax.numpy as jnp
from jax import lax
from jax.experimental import pallas as pl
from jax.experimental.pallas import tpu as pltpu
from jax.sharding import PartitionSpec as P

HD = 72
LEN = 1024
NORM_EPS = 1e-06
LOW = jnp.bfloat16
F32 = jnp.float32
SCALE = HD ** (-0.5)
SCALE_LOG2 = SCALE * math.log2(math.e)
VMEM_LIMIT = 50 * 1024 * 1024
GELU_A = math.sqrt(2 / math.pi)
GELU_B = 0.044715
SHORT = pl.CostEstimate(flops=0, bytes_accessed=0, transcendentals=0)

NN = (((1,), (0,)), ((), ()))
NT = (((1,), (1,)), ((), ()))
TN = (((0,), (0,)), ((), ()))


def dot(left, right, dims=NN):
    return lax.dot_general(left, right, dims, preferred_element_type=F32)


def layer_norm(values, norm_gain, norm_shift):
    centred = values - jnp.mean(values, axis=-1, keepdims=True)
    spread = jnp.mean(centred * centred, axis=-1, keepdims=True)
    return centred * lax.rsqrt(spread + NORM_EPS) * norm_gain + norm_shift


def tie(values, others):
    if not others:
        return values
    return lax.optimization_barrier((*values, *others))[: len(values)]


class Order:
    def __init__(self):
        self.done, self.begun = [], []

    def enter(self, operand):
        return tie((operand,), [*self.done, *self.begun])[0]

    def leave(self, result):
        self.done, self.begun = [result], []


def start_pieces(count, first, table_ref, sources, target_ref, sem):
    rows = target_ref.shape[0] // count

    def each(start):
        for n in range(count):
            slot = table_ref[n]
            for at, source in enumerate(sources):
                @pl.when((slot >= at * first) & (slot < (at + 1) * first))
                def _():
                    copy = pltpu.make_async_copy(
                        source.at[slot - at * first], target_ref.at[pl.ds(n * rows, rows)], sem.at[n]
                    )
                    if start:
                        copy.start()
                    else:
                        copy.wait()

    each(True)
    return functools.partial(each, False)


def spans(parts):
    begin = 0
    for part in parts:
        yield part, pl.ds(begin, part.shape[0])
        begin += part.shape[0]


def moves(pairs, sem, first=0):
    copies = [pltpu.make_async_copy(source, to, sem.at[first + n]) for n, (source, to) in enumerate(pairs)]
    for copy in copies:
        copy.start()
    return [copy.wait for copy in copies]


def load_parts(parts, rows_ref, sem):
    places = [at for _, at in spans(parts)]
    return list(zip(places, moves([(part, rows_ref.at[at]) for part, at in zip(parts, places)], sem)))


def attend_forward_body(heads, n_parts, count, first, table_ref, bias_ref, *refs):
    parts, sources = refs[:n_parts], refs[n_parts:-9]
    qkv_out, mixed_ref, lse_ref, weight_out, qkv_ref, weight_ref, rows_ref, sem, move_sem = refs[-9:]
    wait_pieces = start_pieces(count, first, table_ref, sources, weight_ref, sem)
    loads = load_parts(parts, rows_ref, move_sem)
    cols = heads * HD
    wait_pieces()
    outs = moves([(weight_ref, weight_out)], move_sem, n_parts)
    for at, wait in loads:
        wait()
        qkv_ref[at, :] = (dot(rows_ref[at, :], weight_ref[...]) + bias_ref[...]).astype(LOW)
    outs += moves([(qkv_ref, qkv_out)], move_sem, n_parts + 1)
    for h in range(heads):
        lo = h * HD
        queries = qkv_ref[:, lo : lo + HD]
        keys = qkv_ref[:, cols + lo : cols + lo + HD]
        values = qkv_ref[:, 2 * cols + lo : 2 * cols + lo + HD]
        scores = dot(keys, queries, NT)
        highest = jnp.max(scores, axis=0, keepdims=True)
        probs = jnp.exp2((scores - highest) * SCALE_LOG2)
        total = jnp.sum(probs, axis=0, keepdims=True)
        mixed = dot(values.T, probs.astype(LOW)) / total
        lse_ref[h : h + 1, :] = highest * SCALE_LOG2 + jnp.log2(total)
        mixed_ref[:, lo : lo + HD] = mixed.T.astype(LOW)
    for wait in outs:
        wait()


def kernel_call(body, name, n_vmem, n_any, weight, out_shape, out_any, flops, transcendentals, scratch, n_moves):
    sources, count = weight.sources, weight.count
    shape = sources[0].shape
    moved = sum(math.prod(o.shape) * o.dtype.itemsize for o in out_shape) + 2 * count * shape[1] * shape[2]
    anywhere, inside = pl.BlockSpec(memory_space=pl.ANY), pl.BlockSpec(memory_space=pltpu.VMEM)
    return pl.pallas_call(
        functools.partial(body, count, shape[0]),
        in_specs=[pl.BlockSpec(memory_space=pltpu.SMEM)] + [inside] * n_vmem + [anywhere] * (n_any + len(sources)),
        out_specs=[anywhere if n in out_any else inside for n in range(len(out_shape))],
        out_shape=out_shape,
        scratch_shapes=[
            *(pltpu.VMEM(of.shape, of.dtype) for of in scratch),
            pltpu.SemaphoreType.DMA((count,)),
            pltpu.SemaphoreType.DMA((n_moves,)),
        ],
        compiler_params=pltpu.CompilerParams(vmem_limit_bytes=VMEM_LIMIT),
        cost_estimate=pl.CostEstimate(flops=flops, bytes_accessed=moved, transcendentals=transcendentals),
        name=name,
    )


class Weight:
    def __init__(self, sources, table):
        images, n_dp = table.shape
        _, rows, cols = sources[0].shape
        self.width = n_dp * rows
        if rows % 16:
            whole = jnp.take(jnp.concatenate(sources, axis=0), table.reshape(-1), axis=0)
            sources = (whole.reshape(images, self.width, cols),)
            table = jnp.arange(images, dtype=jnp.int32)[:, None]
        self.sources, self.table, self.count, self.cols = sources, table, table.shape[1], cols
        self.shape = jax.ShapeDtypeStruct((self.width, cols), LOW)


def attend_forward(bias, parts, weight, i, heads):
    cols = heads * HD
    qkv = jax.ShapeDtypeStruct((LEN, 3 * cols), LOW)
    rows = jax.ShapeDtypeStruct((LEN, weight.width), LOW)
    return kernel_call(
        functools.partial(attend_forward_body, heads, len(parts)),
        "attend_forward",
        1,
        len(parts),
        weight,
        [qkv, jax.ShapeDtypeStruct((LEN, cols), LOW), jax.ShapeDtypeStruct((heads, LEN), F32), weight.shape],
        (0, 3),
        heads * LEN * LEN * 1536 + 2 * LEN * weight.width * 3 * cols,
        heads * LEN * LEN,
        [qkv, weight.shape, rows],
        len(parts) + 2,
    )(weight.table[i], bias, *parts, *weight.sources)


def place_body(count, first, table_ref, *refs):
    sources, (weight_ref, sem, _) = refs[:-3], refs[-3:]
    start_pieces(count, first, table_ref, sources, weight_ref, sem)()


def placed(weight, enter, i, name):
    return kernel_call(place_body, name, 0, 0, weight, [weight.shape], (), 0, 0, (), 1)(
        enter(weight.table[i]), *weight.sources
    )[0]


def in_steps(at):
    half = at.size // 2
    return pl.ds(at.start, half), pl.ds(at.start + half, half)


def up_body(n_parts, count, first, table_ref, bias_ref, *refs):
    parts, sources = refs[:n_parts], refs[n_parts:-9]
    act_out, slope_out, weight_out, act_ref, slope_ref, weight_ref, rows_ref, sem, move_sem = refs[-9:]
    wait_pieces = start_pieces(count, first, table_ref, sources, weight_ref, sem)
    loads = load_parts(parts, rows_ref, move_sem)
    wait_pieces()
    outs = moves([(weight_ref, weight_out)], move_sem, n_parts)
    for n, (whole, wait) in enumerate(loads):
        wait()
        for at in in_steps(whole):
            u = dot(rows_ref[at, :], weight_ref[...]) + bias_ref[...]
            square = u * u
            bend = jnp.tanh(u * (GELU_A + GELU_A * GELU_B * square))
            half = 0.5 + 0.5 * bend
            act_ref[at, :] = (u * half).astype(LOW)
            inner = u * (GELU_A + 3 * GELU_A * GELU_B * square)
            slope_ref[at, :] = (half + 0.5 * inner * (1 - bend * bend)).astype(LOW)
        outs += moves(
            [(act_ref.at[whole], act_out.at[whole]), (slope_ref.at[whole], slope_out.at[whole])],
            move_sem,
            n_parts + 1 + 2 * n,
        )
    for wait in outs:
        wait()


def up(bias, parts, weight, i):
    hidden = jax.ShapeDtypeStruct((LEN, weight.cols), LOW)
    rows = jax.ShapeDtypeStruct((LEN, weight.width), LOW)
    return kernel_call(
        functools.partial(up_body, len(parts)), "up", 1, len(parts), weight, [hidden, hidden, weight.shape], (0, 1, 2),
        2 * LEN * weight.width * weight.cols, LEN * weight.cols, [hidden, hidden, weight.shape, rows],
        3 * len(parts) + 1,
    )(weight.table[i], bias, *parts, *weight.sources)


def pre_grad_body(n_parts, count, first, table_ref, slope_in, *refs):
    parts, sources = refs[:n_parts], refs[n_parts:-9]
    grad_out, bias_ref, weight_out, grad_ref, slope_ref, weight_ref, rows_ref, sem, move_sem = refs[-9:]
    wait_pieces = start_pieces(count, first, table_ref, sources, weight_ref, sem)
    loads = load_parts(parts, rows_ref, move_sem)
    slopes = moves([(slope_in.at[at], slope_ref.at[at]) for at, _ in loads], move_sem, n_parts)
    bias_ref[...] = jnp.zeros_like(bias_ref)
    wait_pieces()
    outs = moves([(weight_ref, weight_out)], move_sem, 2 * n_parts)
    for n, (whole, wait) in enumerate(loads):
        wait()
        slopes[n]()
        for at in in_steps(whole):
            grad = (dot(rows_ref[at, :], weight_ref[...]) * slope_ref[at, :].astype(F32)).astype(LOW)
            grad_ref[at, :] = grad
            bias_ref[...] += jnp.sum(grad.astype(F32), axis=0, keepdims=True)
        outs += moves([(grad_ref.at[whole], grad_out.at[whole])], move_sem, 2 * n_parts + 1 + n)
    for wait in outs:
        wait()


def pre_grad(table, slope, parts, weight):
    hidden = jax.ShapeDtypeStruct((LEN, weight.cols), LOW)
    rows = jax.ShapeDtypeStruct((LEN, weight.width), LOW)
    return kernel_call(
        functools.partial(pre_grad_body, len(parts)), "pre_grad", 0, 1 + len(parts), weight,
        [hidden, jax.ShapeDtypeStruct((1, weight.cols), F32), weight.shape], (0, 2),
        2 * LEN * weight.width * weight.cols, 0, [hidden, hidden, weight.shape, rows],
        3 * len(parts) + 1,
    )(table, slope, *parts, *weight.sources)


def attend_backward_body(heads, lse_ref, qkv_in, mixed_in, out_in, *refs):
    parts, (grads_ref, grad_ref, qkv_ref, mixed_ref, out_ref, rows_ref, move_sem) = refs[:-7], refs[-7:]
    cols = heads * HD
    loads = load_parts(parts, rows_ref, move_sem)
    wait_out, wait_qkv, wait_mixed = moves(
        [(out_in, out_ref), (qkv_in, qkv_ref), (mixed_in, mixed_ref)], move_sem, len(parts)
    )
    wait_out()
    for at, wait in loads:
        wait()
        grad_ref[at, :] = dot(rows_ref[at, :], out_ref[...]).astype(LOW)
    wait_qkv()
    wait_mixed()
    for h in range(heads):
        lo = h * HD
        queries = qkv_ref[:, lo : lo + HD]
        keys = qkv_ref[:, cols + lo : cols + lo + HD]
        values = qkv_ref[:, 2 * cols + lo : 2 * cols + lo + HD]
        grads = grad_ref[:, lo : lo + HD]
        products = grads.astype(F32) * mixed_ref[:, lo : lo + HD].astype(F32)
        delta = jnp.sum(products.T, axis=0, keepdims=True)
        probs = jnp.exp2(dot(keys, queries, NT) * SCALE_LOG2 - lse_ref[h : h + 1, :])
        prob_grad = dot(values, grads, NT)
        grads_ref[:, 2 * cols + lo : 2 * cols + lo + HD] = dot(probs.astype(LOW), grads).astype(LOW)
        score_grad = (probs * (prob_grad - delta)).astype(LOW)
        grads_ref[:, cols + lo : cols + lo + HD] = (dot(score_grad, queries) * SCALE).astype(LOW)
        grads_ref[:, lo : lo + HD] = (dot(keys.T, score_grad) * SCALE).T.astype(LOW)


def attend_backward(lse, qkv, mixed, out_full, parts, heads):
    rows, cols = mixed.shape
    return pl.pallas_call(
        functools.partial(attend_backward_body, heads),
        in_specs=[pl.BlockSpec(memory_space=pltpu.VMEM)] + [pl.BlockSpec(memory_space=pl.ANY)] * (3 + len(parts)),
        out_specs=pl.BlockSpec(memory_space=pltpu.VMEM),
        out_shape=jax.ShapeDtypeStruct((rows, 3 * cols), LOW),
        scratch_shapes=[
            pltpu.VMEM((rows, cols), LOW),
            pltpu.VMEM(qkv.shape, LOW),
            pltpu.VMEM(mixed.shape, LOW),
            pltpu.VMEM(out_full.shape, LOW),
            pltpu.VMEM((rows, out_full.shape[0]), LOW),
            pltpu.SemaphoreType.DMA((3 + len(parts),)),
        ],
        compiler_params=pltpu.CompilerParams(vmem_limit_bytes=VMEM_LIMIT),
        cost_estimate=SHORT,
        name="attend_backward",
    )(lse, qkv, mixed, out_full, *parts)


def weight_grad_body(images, n_dp, half, table_ref, *refs):
    lefts, rights, (keep_ref, send_ref, turned, product, sem) = refs[: -5 - images], refs[-5 - images : -5], refs[-5:]
    width = turned.shape[0]
    shard_rows = width // n_dp
    for left, at in spans(lefts):
        turned[:, at] = left[...].T
    step = width // 2

    def piece(start, n):
        slot = table_ref[n]
        source = product.at[n // n_dp, pl.ds((n % n_dp) * shard_rows, shard_rows)]
        for out_ref, mine, index in ((keep_ref, slot < half, slot), (send_ref, slot >= half, slot - half)):
            @pl.when(mine)
            def _():
                copy = pltpu.make_async_copy(source, out_ref.at[index], sem.at[n])
                if start:
                    copy.start()
                else:
                    copy.wait()

    for i in range(images):
        for part in range(2):
            at = pl.ds(part * step, step)
            product[i, at, :] = dot(turned[at, :], rights[i][...]).astype(LOW)
            for d in range(part * n_dp // 2, (part + 1) * n_dp // 2):
                piece(True, i * n_dp + d)
    for n in range(images * n_dp):
        piece(False, n)


def weight_grad(table, lefts, rights, n_dp, name):
    images = len(rights)
    rows, width = LEN, lefts[0].shape[1]
    cols = rights[0].shape[1]
    shard_rows = width // n_dp
    half = images * n_dp // 2
    if shard_rows % 16:
        left = jnp.concatenate(lefts, axis=0)
        whole = jnp.concatenate([dot(left, right, TN).astype(LOW) for right in rights], axis=0)
        slots = whole.reshape(images * n_dp, shard_rows, cols)
        order = jnp.zeros_like(table).at[table].set(jnp.arange(table.shape[0], dtype=jnp.int32))
        slots = jnp.take(slots, order, axis=0)
        return slots[:half], slots[half:]
    shape = jax.ShapeDtypeStruct((half, shard_rows, cols), LOW)
    return pl.pallas_call(
        functools.partial(weight_grad_body, images, n_dp, half),
        in_specs=[pl.BlockSpec(memory_space=pltpu.SMEM)] + [pl.BlockSpec(memory_space=pltpu.VMEM)] * (len(lefts) + images),
        out_specs=[pl.BlockSpec(memory_space=pl.ANY)] * 2,
        out_shape=[shape, shape],
        scratch_shapes=[
            pltpu.VMEM((width, rows), LOW),
            pltpu.VMEM((images, width, cols), LOW),
            pltpu.SemaphoreType.DMA((images * n_dp,)),
        ],
        compiler_params=pltpu.CompilerParams(vmem_limit_bytes=VMEM_LIMIT),
        cost_estimate=SHORT,
        name=name,
    )(table, *lefts, *rights)


class Plan:
    def __init__(self, n_dp, n_t, ranks):
        self.n_dp, self.n_t, self.ranks = n_dp, n_t, ranks
        self.images = n_t // ranks
        dims = [("dp", 1 << b) for b in reversed(range(n_dp.bit_length() - 1))]
        image_dims = [("image", 1 << b) for b in reversed(range(self.images.bit_length() - 1))]
        even = dims + image_dims
        odd = list(even)
        if image_dims and dims:
            odd[-2], odd[-1] = odd[-1], odd[-2]
        self.orders = {"far": (even, odd), "near": tuple(way[-2:-1] + way[:-2] + way[-1:] for way in (even, odd))}
        self.stages = len(even)
        self.rank_stages = ranks.bit_length() - 1

    def permute(self, values, partner):
        pairs = []
        for d in range(self.n_dp):
            for t in range(self.n_t):
                d2, i2, r2 = partner(d, t // self.ranks, t % self.ranks)
                pairs.append((d * self.n_t + t, d2 * self.n_t + i2 * self.ranks + r2))
        return lax.ppermute(values, ("dp", "tensor"), pairs)

    def exchange(self, values, stage, way="far"):
        def partner(d, i, r):
            kind, step = self.orders[way][r & 1][stage]
            return (d ^ step, i, r) if kind == "dp" else (d, i ^ step, r)

        return self.permute(values, partner)

    def rank_exchange(self, values, stage):
        return self.permute(values, lambda d, i, r: (d, i, r ^ (1 << stage)))

    def slots(self, way="far"):
        me_dp, me_t = lax.axis_index("dp"), lax.axis_index("tensor")
        flips = jnp.arange(self.n_dp, dtype=jnp.int32)[None, :] ^ me_dp
        images = jnp.arange(self.images, dtype=jnp.int32)[:, None]

        def table(order):
            total = jnp.zeros((self.images, self.n_dp), jnp.int32)
            for stage, (kind, step) in enumerate(order):
                source = flips if kind == "dp" else images
                total = total + jnp.where((source & step) != 0, 1 << stage, 0)
            return total

        even, odd = self.orders[way]
        return jnp.where((me_t % self.ranks) & 1, table(odd), table(even))

    def rank_gather(self, shard):
        parts = [shard]
        for stage in range(self.rank_stages):
            mine = jnp.concatenate(parts, axis=0) if stage else shard
            parts.append(self.rank_exchange(mine, stage))
        return parts

    def rank_scatter(self, rows, *after):
        for stage in reversed(range(self.rank_stages)):
            half = rows.shape[0] // 2
            (theirs,) = tie((self.rank_exchange(rows[half:].astype(LOW), stage),), after)
            rows = rows[:half] + theirs.astype(F32)
        return rows


class Gather:
    def __init__(self, plan, order, shard, way="far"):
        self.plan, self.order, self.held, self.stage, self.way = plan, order, (shard[None],), 0, way

    def to(self, stage, *after):
        while self.stage < stage:
            held = tie(self.held, [*self.order.done, *after])
            mine = held[0] if len(held) == 1 else jnp.concatenate(held, axis=0)
            self.held = (mine, self.plan.exchange(mine, self.stage, self.way))
            self.order.begun.append(mine)
            self.stage += 1
        return self.held[-1]

    def weight(self):
        self.to(self.plan.stages)
        return Weight(self.held, self.plan.slots(self.way))


class Scatter:
    def __init__(self, plan, order, keep, send, way):
        self.plan, self.order, self.keep, self.send, self.way = plan, order, keep, send, way
        self.theirs, self.stage = None, plan.stages

    def total(self, part):
        return self.keep[part].astype(F32) + self.theirs[part].astype(F32)

    def to(self, stage, *after):
        while self.stage > stage:
            if self.theirs is not None:
                self.keep, self.theirs = tie((self.keep, self.theirs), [*self.order.done, *after])
                half = self.keep.shape[0] // 2
                self.send, self.keep = self.total(slice(half, None)).astype(LOW), self.total(slice(half)).astype(LOW)
            self.stage -= 1
            self.theirs = self.plan.exchange(self.send, self.stage, self.way)
            self.order.begun.append(self.send)
        return self.theirs

    def finish(self):
        self.to(0)
        return self.total(0)


def local(
    tokens, gain_one, shift_one, w_query, b_query, w_key, w_value, b_value, w_out, b_out,
    gain_two, shift_two, w_up, b_up, w_down, b_down, cotangent, plan=None,
):
    images, ranks, n_dp = plan.images, plan.ranks, plan.n_dp
    shard_rows = w_query.shape[0]
    width = tokens.shape[1]
    head_cols, hidden_cols = w_query.shape[1], w_up.shape[1]
    heads = head_cols // HD
    me_t = lax.axis_index("tensor")
    me_image, me_rank = me_t // ranks, me_t % ranks

    def shard_of(i):
        return (me_image ^ i) * ranks + me_rank

    def columns(vector, cols):
        return [lax.dynamic_slice_in_dim(vector, shard_of(i) * cols, cols) for i in range(images)]

    def uncolumns(parts, length):
        cols = parts[0].shape[0]
        blank = jnp.zeros((length,), F32)
        for i in range(images):
            blank = lax.dynamic_update_slice_in_dim(blank, parts[i], shard_of(i) * cols, 0)
        return blank

    order = Order()

    def scatter(lefts, rights, name, way="far"):
        table = plan.slots(way).reshape(-1)
        keep, send = weight_grad(order.enter(table), lefts, rights, n_dp, name)
        order.leave(send)
        begun = Scatter(plan, order, keep, send, way)
        begun.to(plan.stages - 1)
        return begun

    def low(values):
        return values.astype(LOW)

    each = range(images)
    last, near = plan.stages, max(plan.stages - 1, 0)
    far = max(plan.stages - 2, 0)
    first = max(plan.stages - 3, 0)
    gather_qkv = Gather(plan, order, jnp.concatenate([low(w_query), low(w_key), low(w_value)], axis=1))
    gather_out = Gather(plan, order, low(w_out).T)
    gather_up = Gather(plan, order, low(w_up))
    gather_down = Gather(plan, order, low(w_down).T, "near")
    cot_rows = plan.rank_gather(cotangent)
    inputs32 = tokens.astype(F32)
    normed_one = low(layer_norm(inputs32, gain_one, shift_one))
    rows_one = plan.rank_gather(normed_one)
    token = gather_qkv.to(first)
    down_token = gather_down.to(min(1, far))
    gather_qkv.to(far)
    out_token = gather_out.to(first, token)
    token = gather_qkv.held[-1]
    gather_qkv.to(near, out_token, down_token, rows_one[-1], cot_rows[-1])
    up_token = gather_up.to(first, token)
    out_token = gather_out.to(far, token)
    token = gather_qkv.held[-1]
    gather_qkv.to(last, out_token, up_token)
    gather_up.to(far, token)
    gather_out.to(near, gather_qkv.held[-1])
    gather_up.to(near, gather_qkv.held[-1])
    gather_down.to(near - 1, gather_up.held[0])
    order.begun = [gather_up.held[0], gather_down.held[0]]

    query_bias, value_bias = columns(b_query, head_cols), columns(b_value, head_cols)
    blank = jnp.zeros((head_cols,), F32)
    qkv, mixed, lse, qkv_full = [None] * images, [None] * images, [None] * images, [None] * images
    for i in each:
        bias = order.enter(jnp.concatenate([query_bias[i], blank, value_bias[i]])[None])
        qkv[i], mixed[i], lse[i], qkv_full[i] = attend_forward(bias, rows_one, gather_qkv.weight(), i, heads)
        order.leave(lse[i])
        if i == 0:
            gather_out.to(last)
            gather_up.to(last)
            gather_down.to(near)
    gather_down.to(last)

    out_full = [placed(gather_out.weight(), order.enter, i, "place_out") for i in each]
    down_held = [] if gather_down.stage < last else [gather_down.held[0]]
    attn = sum(dot(mixed[i], out_full[i], NT) for i in each)
    (attn,) = tie((attn,), down_held)
    residual = inputs32 + plan.rank_scatter(attn, gather_up.held[-1]) + b_out
    normed_two = low(layer_norm(residual, gain_two, shift_two))
    order.leave(normed_two[:8])
    rows_two = plan.rank_gather(normed_two)
    up_bias = columns(b_up, hidden_cols)
    act, slope, up_full = [None] * images, [None] * images, [None] * images
    for i in each:
        bias = order.enter(up_bias[i][None])
        act[i], slope[i], up_full[i] = up(bias, rows_two, gather_up.weight(), i)
        order.leave(act[i])
    scatter_down = scatter(cot_rows, act, "grad_down", "near")

    grad_out = cotangent.astype(F32)
    down_bias_grad = jnp.sum(grad_out, axis=0)
    pre_low, up_bias_parts, down_full = [None] * images, [None] * images, [None] * images
    down_weight = gather_down.weight()
    for i in each:
        table = order.enter(down_weight.table[i])
        pre_low[i], up_bias_parts[i], down_full[i] = pre_grad(table, slope[i], cot_rows, down_weight)
        order.leave(up_bias_parts[i])
    partial_two = sum(dot(pre_low[i], up_full[i], NT) for i in each)
    order.leave(partial_two[:8])
    scatter_up = scatter(rows_two, pre_low, "grad_up")
    scatter_down.to(far)
    (partial_two,) = tie((partial_two,), [scatter_down.send])
    norm_two_grad = plan.rank_scatter(partial_two)
    _, pull_two = jax.vjp(layer_norm, residual, gain_two, shift_two)
    residual_part, gain_two_grad, shift_two_grad = pull_two(norm_two_grad)
    residual_grad = grad_out + residual_part
    branch_low = low(residual_grad)
    out_bias_grad = jnp.sum(branch_low, axis=0, dtype=F32)
    branch_rows = plan.rank_gather(branch_low)
    scatter_out = scatter(branch_rows, mixed, "grad_out")

    qkv_grads = []
    for i in each:
        start = order.enter(lse[i])
        qkv_grads.append(attend_backward(start, qkv[i], mixed[i], out_full[i], branch_rows, heads))
        order.leave(qkv_grads[i])
        if i == 0:
            scatter_down.to(first)
            scatter_up.to(far)
            scatter_out.to(far)
    scatter_qkv = scatter(rows_one, qkv_grads, "grad_qkv")
    scatter_up.to(first)
    scatter_out.to(first)
    scatter_down.to(0)
    partial_one = sum(dot(order.enter(qkv_grads[i]), qkv_full[i], NT) for i in each)
    order.leave(partial_one[:8])
    mlp = sum(dot(order.enter(act[i]), down_full[i], NT) for i in each)
    order.leave(mlp[:8])
    scatter_up.to(0)
    scatter_out.to(0)
    norm_one_grad = order.enter(plan.rank_scatter(partial_one))
    _, pull_one = jax.vjp(layer_norm, inputs32, gain_one, shift_one)
    input_part, gain_one_grad, shift_one_grad = pull_one(norm_one_grad)
    grad_tokens = low(residual_grad + input_part)
    output = low(residual + plan.rank_scatter(mlp) + b_down)
    order.leave(gain_one_grad)
    scatter_qkv.to(far)
    gain_one_grad = order.enter(gain_one_grad)
    down_grad = scatter_down.finish().T
    up_grad = scatter_up.finish()
    out_grad = scatter_out.finish().T
    qkv_sums = [jnp.sum(grads, axis=0, dtype=F32) for grads in qkv_grads]
    up_bias_grad = uncolumns([order.enter(part)[0] for part in up_bias_parts], b_up.shape[0])
    query_bias_grad = uncolumns([sums[:head_cols] for sums in qkv_sums], b_query.shape[0])
    value_bias_grad = uncolumns([sums[2 * head_cols :] for sums in qkv_sums], b_value.shape[0])

    vectors = [
        gain_one_grad, shift_one_grad, query_bias_grad, value_bias_grad, out_bias_grad,
        gain_two_grad, shift_two_grad, up_bias_grad, down_bias_grad,
    ]
    lengths = [vector.shape[0] for vector in vectors]
    together = jnp.concatenate([*vectors, jnp.zeros((-sum(lengths) % 1024,), F32)])
    for stage in range(plan.rank_stages):
        together = together + plan.rank_exchange(together, stage)
    for stage in range(plan.stages):
        together = together + plan.exchange(together, stage)
        if stage in (first, near):
            order.leave(together)
            if stage == first:
                scatter_qkv.to(first, up_grad, out_grad)
            else:
                scatter_qkv.to(0)
            together = order.enter(together)
    qkv_grad = scatter_qkv.finish()
    query_grad, key_grad, value_grad = (qkv_grad[:, n * head_cols : (n + 1) * head_cols] for n in range(3))
    small, begin = [], 0
    for length in lengths:
        small.append(together[begin : begin + length])
        begin += length
    return (
        output, grad_tokens, small[0], small[1], query_grad, small[2], key_grad, value_grad, small[3],
        out_grad, small[4], small[5], small[6], up_grad, small[7], down_grad, small[8],
    )


def solution(mesh):
    split = P(("dp", "tensor"), None)
    whole, wide, tall = P(), P("dp", "tensor"), P("tensor", "dp")
    n_dp, n_t = mesh.shape["dp"], mesh.shape["tensor"]

    def layer(*args):
        rows = args[0].shape[0] // (n_dp * n_t)
        plan = Plan(n_dp, n_t, LEN // rows)
        return jax.shard_map(
            functools.partial(local, plan=plan),
            mesh=mesh,
            in_specs=(
                split, whole, whole, wide, whole, wide, wide, whole, tall, whole,
                whole, whole, wide, whole, tall, whole, split,
            ),
            out_specs=(
                split, split, whole, whole, wide, whole, wide, wide, whole,
                tall, whole, whole, whole, wide, whole, tall, whole,
            ),
            check_vma=False,
        )(*args)

    return layer
```

profile of v0, /device:TPU:0, one launch (start us, length us, event | category | flops | bytes accessed | tf_op | source)
XLA Modules:
  0.0 387.2 jit_solution(2568459073037327624)
XLA Ops:
  3.8 4.1 %collective-permute-start = (bf16[1,144,864]{2,1,0:T(8,128)(2,1)S(1)}, bf16[1,144,864]{2,1,0:T(8,128)(2,1)S(1)}, u32[]{:S(2)}, u32[]{:S(2)}) collective-permute-start(bf16[1,144,864]{2,1,0:T(8,128)(2,1)S(1)} %maximum_bitcast_fusion), channel_id=1, source_target_pairs={{0,16},{1,17},{2,18},{3,19},{4,20},{5,21},{6,22},{7,23},{8,24},{9,... | collective-permute-start | bytes 746504 | tf_op jit(solution)/shard_map/ppermute | solution.py:390
  10.3 9.3 %collective-permute-done = bf16[1,144,864]{2,1,0:T(8,128)(2,1)S(1)} collective-permute-done((bf16[1,144,864]{2,1,0:T(8,128)(2,1)S(1)}, bf16[1,144,864]{2,1,0:T(8,128)(2,1)S(1)}, u32[]{:S(2)}, u32[]{:S(2)}) %collective-permute-start) | collective-permute-done | bytes 248864 | tf_op jit(solution)/shard_map/ppermute | solution.py:390
  22.2 3.4 collective-permute-start.3
  27.8 6.3 %collective-permute-done.3 = bf16[1,144,288]{2,1,0:T(8,128)(2,1)S(1)} collective-permute-done((bf16[1,144,288]{2,1,0:T(8,128)(2,1)S(1)}, bf16[1,144,288]{2,1,0:T(8,128)(2,1)S(1)}, u32[]{:S(2)}, u32[]{:S(2)}) %collective-permute-start.3) | collective-permute-done | bytes 82976 | tf_op jit(solution)/shard_map/ppermute | solution.py:390
  43.5 8.5 %collective-permute-done.9 = bf16[2,144,288]{2,1,0:T(8,128)(2,1)S(1)} collective-permute-done((bf16[2,144,288]{2,1,0:T(8,128)(2,1)S(1)}, bf16[2,144,288]{2,1,0:T(8,128)(2,1)S(1)}, u32[]{:S(2)}, u32[]{:S(2)}) %collective-permute-start.9) | collective-permute-done | bytes 165920 | tf_op jit(solution)/shard_map/ppermute | solution.py:390
  62.1 14.6 %collective-permute-done.8 = bf16[2,144,1076]{2,1,0:T(8,128)(2,1)S(1)} collective-permute-done((bf16[2,144,1076]{2,1,0:T(8,128)(2,1)S(1)}, bf16[2,144,1076]{2,1,0:T(8,128)(2,1)S(1)}, u32[]{:S(2)}, u32[]{:S(2)}) %collective-permute-start.8) | collective-permute-done | bytes 619808 | tf_op jit(solution)/shard_map/ppermute | solution.py:390
  76.7 6.6 %collective-permute-done.10.refs_3_ = bf16[8,144,864]{2,1,0:T(8,128)(2,1)} collective-permute-done((bf16[8,144,864]{2,1,0:T(8,128)(2,1)}, bf16[8,144,864]{2,1,0:T(8,128)(2,1)}, u32[]{:S(2)}, u32[]{:S(2)}) %collective-permute-start.10) | collective-permute-done | bytes 1990688 | tf_op jit(solution)/shard_map/ppermute | solution.py:390
  87.8 11.5 %attend_forward.2 = (bf16[1024,864]{1,0:T(8,128)(2,1)}, bf16[1024,288]{1,0:T(8,128)(2,1)S(1)}, f32[4,1024]{1,0:T(4,128)S(1)}, bf16[1152,864]{1,0:T(8,128)(2,1)}) custom-call(s32[8]{0:T(128)S(1)} %get-tuple-element.147.table_ref, f32[1,864]{1,0:T(1,128)S(1)} %broadcast_in_dim.276.bias_ref, bf16[512,1152]{1,0:T(8,128)(2,1)S(1)} %fusion.7.refs_0_, ...), custom_call_target="tpu_custom_call" | custom-call | flops 8480882688 | bytes 6356992 | tf_op jit(solution)/shard_map/attend_forward/pallas_call | solution.py:161
  99.4 7.1 %collective-permute-done.11 = bf16[4,144,288]{2,1,0:T(8,128)(2,1)S(1)} collective-permute-done((bf16[4,144,288]{2,1,0:T(8,128)(2,1)S(1)}, bf16[4,144,288]{2,1,0:T(8,128)(2,1)S(1)}, u32[]{:S(2)}, u32[]{:S(2)}) %collective-permute-start.11) | collective-permute-done | bytes 331808 | tf_op jit(solution)/shard_map/ppermute | solution.py:390
  107.4 5.8 %collective-permute-done.13 = bf16[2,144,1076]{2,1,0:T(8,128)(2,1)S(1)} collective-permute-done((bf16[2,144,1076]{2,1,0:T(8,128)(2,1)S(1)}, bf16[2,144,1076]{2,1,0:T(8,128)(2,1)S(1)}, u32[]{:S(2)}, u32[]{:S(2)}) %collective-permute-start.13) | collective-permute-done | bytes 619808 | tf_op jit(solution)/shard_map/ppermute | solution.py:390
  118.3 11.5 %attend_forward.3 = (bf16[1024,864]{1,0:T(8,128)(2,1)}, bf16[1024,288]{1,0:T(8,128)(2,1)S(1)}, f32[4,1024]{1,0:T(4,128)S(1)}, bf16[1152,864]{1,0:T(8,128)(2,1)}) custom-call(s32[8]{0:T(128)S(1)} %get-tuple-element.149.table_ref, f32[1,864]{1,0:T(1,128)S(1)} %broadcast_in_dim.281.bias_ref, bf16[512,1152]{1,0:T(8,128)(2,1)S(1)} %fusion.7.refs_0_, ...), custom_call_target="tpu_custom_call" | custom-call | flops 8480882688 | bytes 6356992 | tf_op jit(solution)/shard_map/attend_forward/pallas_call | solution.py:161
  129.8 13.6 %collective-permute-done.14 = bf16[4,144,1076]{2,1,0:T(8,128)(2,1)S(1)} collective-permute-done((bf16[4,144,1076]{2,1,0:T(8,128)(2,1)S(1)}, bf16[4,144,1076]{2,1,0:T(8,128)(2,1)S(1)}, u32[]{:S(2)}, u32[]{:S(2)}) %collective-permute-start.14) | collective-permute-done | bytes 1239584 | tf_op jit(solution)/shard_map/ppermute | solution.py:390
  162.3 9.3 %up.2 = (bf16[1024,1076]{1,0:T(8,128)(2,1)}, bf16[1024,1076]{1,0:T(8,128)(2,1)}, bf16[1152,1076]{1,0:T(8,128)(2,1)}) custom-call(s32[8]{0:T(128)S(1)} %copy-done.21, f32[1,1076]{1,0:T(1,128)S(1)} %broadcast_in_dim.282.bias_ref, bf16[512,1152]{1,0:T(8,128)(2,1)} %add_convert_fusion.5.refs_0_, bf16[512,1152]{1,0:T(8,128)(2,1)} %collective-permute-done.18.refs_1_, ...), custom_call_target="tpu_custom_call" | custom-call | flops 2538602496 | bytes 9365504 | tf_op jit(solution)/shard_map/up/pallas_call | solution.py:221
  171.6 9.9 %up.3 = (bf16[1024,1076]{1,0:T(8,128)(2,1)}, bf16[1024,1076]{1,0:T(8,128)(2,1)}, bf16[1152,1076]{1,0:T(8,128)(2,1)}) custom-call(s32[8]{0:T(128)S(1)} %copy-done.19, f32[1,1076]{1,0:T(1,128)S(1)} %broadcast_in_dim.283.bias_ref, bf16[512,1152]{1,0:T(8,128)(2,1)} %add_convert_fusion.5.refs_0_, bf16[512,1152]{1,0:T(8,128)(2,1)} %collective-permute-done.18.refs_1_, ...), custom_call_target="tpu_custom_call" | custom-call | flops 2538602496 | bytes 9365504 | tf_op jit(solution)/shard_map/up/pallas_call | solution.py:221
  181.5 10.0 %grad_down.1 = (bf16[8,144,1076]{2,1,0:T(8,128)(2,1)}, bf16[8,144,1076]{2,1,0:T(8,128)(2,1)}) custom-call(s32[16]{0:T(128)S(1)} %select_n.272.table_ref, bf16[512,1152]{1,0:T(8,128)(2,1)S(1)} %copy-done, bf16[512,1152]{1,0:T(8,128)(2,1)S(1)} %collective-permute-done.6.refs_1_, bf16[1024,1076]{1,0:T(8,128)(2,1)} %get-tuple-element.197.refs_2_, ...), custom_call_target="tpu_custom_call" | custom-call | tf_op jit(solution)/shard_map/grad_down/pallas_call | solution.py:354
  193.4 7.6 %pre_grad.2 = (bf16[1024,1076]{1,0:T(8,128)(2,1)}, f32[1,1076]{1,0:T(1,128)S(1)}, bf16[1152,1076]{1,0:T(8,128)(2,1)}) custom-call(s32[8]{0:T(128)S(1)} %get-tuple-element.157.table_ref, bf16[1024,1076]{1,0:T(8,128)(2,1)} %get-tuple-element.158.slope_in, bf16[512,1152]{1,0:T(8,128)(2,1)S(1)} %copy-done, bf16[512,1152]{1,0:T(8,128)(2,1)S(1)} %collective-permute-done.6.refs_1_, ...), custom_call_target="tpu_custom_call" | custom-call | flops 2538602496 | bytes 7166160 | tf_op jit(solution)/shard_map/pre_grad/pallas_call | solution.py:252
  201.0 7.7 %pre_grad.3 = (bf16[1024,1076]{1,0:T(8,128)(2,1)}, f32[1,1076]{1,0:T(1,128)S(1)}, bf16[1152,1076]{1,0:T(8,128)(2,1)}) custom-call(s32[8]{0:T(128)S(1)} %get-tuple-element.161.table_ref, bf16[1024,1076]{1,0:T(8,128)(2,1)} %get-tuple-element.162.slope_in, bf16[512,1152]{1,0:T(8,128)(2,1)S(1)} %copy-done, bf16[512,1152]{1,0:T(8,128)(2,1)S(1)} %collective-permute-done.6.refs_1_, ...), custom_call_target="tpu_custom_call" | custom-call | flops 2538602496 | bytes 7166160 | tf_op jit(solution)/shard_map/pre_grad/pallas_call | solution.py:252
  208.7 10.8 %grad_up.1 = (bf16[8,144,1076]{2,1,0:T(8,128)(2,1)}, bf16[8,144,1076]{2,1,0:T(8,128)(2,1)}) custom-call(s32[16]{0:T(128)S(1)} %select_n.266.table_ref, bf16[512,1152]{1,0:T(8,128)(2,1)} %add_convert_fusion.5.refs_0_, bf16[512,1152]{1,0:T(8,128)(2,1)} %collective-permute-done.18.refs_1_, bf16[1024,1076]{1,0:T(8,128)(2,1)} %get-tuple-element.159.refs_2_, ...), custom_call_target="tpu_custom_call" | custom-call | tf_op jit(solution)/shard_map/grad_up/pallas_call | solution.py:354
  219.6 3.5 fusion.36
  223.1 4.1 %convolution_add_fusion.3 = f32[1024,1152]{1,0:T(8,128)S(1)} fusion(f32[1024,1152]{1,0:T(8,128)S(1)} %fusion.36, bf16[1024,1076]{1,0:T(8,128)(2,1)S(1)} %copy-done.42, bf16[1152,1076]{1,0:T(8,128)(2,1)S(1)} %copy-done.82), kind=kOutput, calls=%fused_computation.3 | convolution fusion | flops 2539782144 | bytes 14119936 | tf_op jit(solution)/shard_map/dot_general | solution.py:29
  227.2 3.5 add_convert_fusion.2
  241.1 7.4 %grad_out.1 = (bf16[8,144,288]{2,1,0:T(8,128)(2,1)S(1)}, bf16[8,144,288]{2,1,0:T(8,128)(2,1)S(1)}) custom-call(s32[16]{0:T(128)S(1)} %select_n.266.table_ref, bf16[512,1152]{1,0:T(8,128)(2,1)} %copy-done.1, bf16[512,1152]{1,0:T(8,128)(2,1)} %copy-done.3, bf16[1024,288]{1,0:T(8,128)(2,1)S(1)} %copy-done.10, bf16[1024,288]{1,0:T(8,128)(2,1)S(1)} %copy-done.8), custom_call_target="tpu_custom_call" | custom-call | tf_op jit(solution)/shard_map/grad_out/pallas_call | solution.py:354
  251.9 14.8 %attend_backward.2.refs_2_ = bf16[1024,864]{1,0:T(8,128)(2,1)} custom-call(f32[4,1024]{1,0:T(4,128)S(1)} %copy-done.17, bf16[1024,864]{1,0:T(8,128)(2,1)} %get-tuple-element.174.qkv_in, bf16[1024,288]{1,0:T(8,128)(2,1)S(1)} %copy-done.10, bf16[1152,288]{1,0:T(8,128)(2,1)S(1)} %copy-done.6, bf16[512,1152]{1,0:T(8,128)(2,1)S(1)} %copy-done.2, ...), custom_call_target="tpu_custom_call" | custom-call | tf_op jit(solution)/shard_map/attend_backward/pallas_call | solution.py:291
  266.7 4.3 %add_convert_fusion = (bf16[4,144,1076]{2,1,0:T(8,128)(2,1)}, bf16[4,144,1076]{2,1,0:T(8,128)(2,1)}) fusion(bf16[8,144,1076]{2,1,0:T(8,128)(2,1)} %collective-permute-done.24, bf16[8,144,1076]{2,1,0:T(8,128)(2,1)S(1)} %copy-done.36), kind=kLoop, calls=%fused_computation.19 | loop fusion | flops 4958208 | bytes 7437312 | tf_op jit(solution)/shard_map/convert_element_type | solution.py:463
  273.1 3.4 collective-permute-start.28
  278.9 14.6 %attend_backward.3.refs_3_ = bf16[1024,864]{1,0:T(8,128)(2,1)} custom-call(f32[4,1024]{1,0:T(4,128)S(1)} %get-tuple-element.183.lse_ref, bf16[1024,864]{1,0:T(8,128)(2,1)} %get-tuple-element.184.qkv_in, bf16[1024,288]{1,0:T(8,128)(2,1)S(1)} %copy-done.8, bf16[1152,288]{1,0:T(8,128)(2,1)S(1)} %place_out.3.out_in, bf16[512,1152]{1,0:T(8,128)(2,1)S(1)} %copy-done.2, ...), custom_call_target="tpu_custom_call" | custom-call | tf_op jit(solution)/shard_map/attend_backward/pallas_call | solution.py:291
  293.6 8.6 %grad_qkv.1 = (bf16[8,144,864]{2,1,0:T(8,128)(2,1)}, bf16[8,144,864]{2,1,0:T(8,128)(2,1)}) custom-call(s32[16]{0:T(128)S(1)} %select_n.266.table_ref, bf16[512,1152]{1,0:T(8,128)(2,1)S(1)} %copy-done.12, bf16[512,1152]{1,0:T(8,128)(2,1)S(1)} %copy-done.15, bf16[1024,864]{1,0:T(8,128)(2,1)} %attend_backward.2.refs_2_, bf16[1024,864]{1,0:T(8,128)(2,1)} %attend_backward.3.refs_3_), custom_call_target="tpu_custom_call" | custom-call | tf_op jit(solution)/shard_map/grad_qkv/pallas_call | solution.py:354
  316.1 3.6 fusion.38
  319.7 5.6 %convolution_add_fusion.2 = f32[1024,1152]{1,0:T(8,128)} fusion(f32[1024,1152]{1,0:T(8,128)S(1)} %fusion.38, bf16[1024,1076]{1,0:T(8,128)(2,1)S(1)} %copy-done.40, bf16[1152,1076]{1,0:T(8,128)(2,1)S(1)} %copy-done.80), kind=kOutput, calls=%fused_computation.2 | convolution fusion | flops 2539782144 | bytes 14119936 | tf_op jit(solution)/shard_map/dot_general | solution.py:29
  328.1 5.1 %collective-permute-done.31 = bf16[2,144,1076]{2,1,0:T(8,128)(2,1)S(1)} collective-permute-done((bf16[2,144,1076]{2,1,0:T(8,128)(2,1)S(1)}, bf16[2,144,1076]{2,1,0:T(8,128)(2,1)S(1)}, u32[]{:S(2)}, u32[]{:S(2)}) %collective-permute-start.31) | collective-permute-done | bytes 619808 | tf_op jit(solution)/shard_map/ppermute | solution.py:390
  367.7 5.5 %collective-permute-done.42 = bf16[2,144,864]{2,1,0:T(8,128)(2,1)S(1)} collective-permute-done((bf16[2,144,864]{2,1,0:T(8,128)(2,1)S(1)}, bf16[2,144,864]{2,1,0:T(8,128)(2,1)S(1)}, u32[]{:S(2)}, u32[]{:S(2)}) %collective-permute-start.42) | collective-permute-done | bytes 497696 | tf_op jit(solution)/shard_map/ppermute | solution.py:390
  377.3 8.6 %collective-permute-done.43 = bf16[1,144,864]{2,1,0:T(8,128)(2,1)S(1)} collective-permute-done((bf16[1,144,864]{2,1,0:T(8,128)(2,1)S(1)}, bf16[1,144,864]{2,1,0:T(8,128)(2,1)S(1)}, u32[]{:S(2)}, u32[]{:S(2)}) %collective-permute-start.43) | collective-permute-done | bytes 248864 | tf_op jit(solution)/shard_map/ppermute | solution.py:390
  (369 shorter events, 134.7 us)
Async XLA Ops:
  3.8 15.8 %collective-permute-start = (bf16[1,144,864]{2,1,0:T(8,128)(2,1)S(1)}, bf16[1,144,864]{2,1,0:T(8,128)(2,1)S(1)}, u32[]{:S(2)}, u32[]{:S(2)}) collective-permute-start(bf16[1,144,864]{2,1,0:T(8,128)(2,1)S(1)} %maximum_bitcast_fusion), channel_id=1, source_target_pairs={{0,16},{1,17},{2,18},{3,19},{4,20},{5,21},{6,22},{7,23},{8,24},{9,... | collective-permute-start | bytes 746504 | tf_op jit(solution)/shard_map/ppermute | solution.py:390
  9.8 25.3 %collective-permute-start.5 = (bf16[512,1152]{1,0:T(8,128)(2,1)S(1)}, bf16[512,1152]{1,0:T(8,128)(2,1)S(1)}, u32[]{:S(2)}, u32[]{:S(2)}) collective-permute-start(bf16[512,1152]{1,0:T(8,128)(2,1)S(1)} %fusion.7.refs_0_), channel_id=1, source_target_pairs={{0,1},{1,0},{2,3},{3,2},{4,5},{5,4},{6,7},{7,6},{8,9},{9,8},{10,11... | collective-permute-start | bytes 3538952 | tf_op jit(solution)/shard_map/ppermute | solution.py:390
  9.9 26.3 %collective-permute-start.6 = (bf16[512,1152]{1,0:T(8,128)(2,1)S(1)}, bf16[512,1152]{1,0:T(8,128)(2,1)S(1)}, u32[]{:S(2)}, u32[]{:S(2)}) collective-permute-start(bf16[512,1152]{1,0:T(8,128)(2,1)S(1)} %copy-done), channel_id=1, source_target_pairs={{0,1},{1,0},{2,3},{3,2},{4,5},{5,4},{6,7},{7,6},{8,9},{9,8},{10,11... | collective-permute-start | bytes 3538952 | tf_op jit(solution)/shard_map/ppermute | solution.py:390
  19.7 15.4 %collective-permute-start.1 = (bf16[2,144,864]{2,1,0:T(8,128)(2,1)S(1)}, bf16[2,144,864]{2,1,0:T(8,128)(2,1)S(1)}, u32[]{:S(2)}, u32[]{:S(2)}) collective-permute-start(bf16[2,144,864]{2,1,0:T(8,128)(2,1)S(1)} %pad_maximum_fusion), channel_id=1, source_target_pairs={{0,8},{1,9},{2,10},{3,11},{4,12},{5,13},{6,14},{7,15},{8,0},{9,1},... | collective-permute-start | bytes 1493000 | tf_op jit(solution)/shard_map/ppermute | solution.py:390
  36.3 19.0 %collective-permute-start.7 = (bf16[4,144,864]{2,1,0:T(8,128)(2,1)S(1)}, bf16[4,144,864]{2,1,0:T(8,128)(2,1)S(1)}, u32[]{:S(2)}, u32[]{:S(2)}) collective-permute-start(bf16[4,144,864]{2,1,0:T(8,128)(2,1)S(1)} %constant_dynamic-update-slice_fusion), channel_id=1, source_target_pairs={{0,4},{1,3},{2,6},{3,1},{4,0},{5,7},{6,2},{7,5},{8,12},{9,11},{10,... | collective-permute-start | bytes 2985992 | tf_op jit(solution)/shard_map/ppermute | solution.py:390
  38.3 16.9 %collective-permute-start.2 = (bf16[1,144,1076]{2,1,0:T(8,128)(2,1)}, bf16[1,144,1076]{2,1,0:T(8,128)(2,1)}, u32[]{:S(2)}, u32[]{:S(2)}) collective-permute-start(bf16[1,144,1076]{2,1,0:T(8,128)(2,1)} %convert_bitcast_fusion.1), channel_id=1, source_target_pairs={{0,16},{1,17},{2,18},{3,19},{4,20},{5,21},{6,22},{7,23},{8,24},{9,... | collective-permute-start | bytes 929672 | tf_op jit(solution)/shard_map/ppermute | solution.py:390
  57.3 26.0 %collective-permute-start.10 = (bf16[8,144,864]{2,1,0:T(8,128)(2,1)}, bf16[8,144,864]{2,1,0:T(8,128)(2,1)}, u32[]{:S(2)}, u32[]{:S(2)}) collective-permute-start(bf16[8,144,864]{2,1,0:T(8,128)(2,1)} %constant_dynamic-update-slice_fusion.6.refs_2_), channel_id=1, source_target_pairs={{0,2},{1,5},{2,0},{3,7},{4,6},{5,1},{6,4},{7,3},{8,10},{9,13},{10,... | collective-permute-start | bytes 5971976 | tf_op jit(solution)/shard_map/ppermute | solution.py:390
  60.1 16.6 %collective-permute-start.8 = (bf16[2,144,1076]{2,1,0:T(8,128)(2,1)S(1)}, bf16[2,144,1076]{2,1,0:T(8,128)(2,1)S(1)}, u32[]{:S(2)}, u32[]{:S(2)}) collective-permute-start(bf16[2,144,1076]{2,1,0:T(8,128)(2,1)S(1)} %constant_dynamic-update-slice_fusion.2), channel_id=1, source_target_pairs={{0,8},{1,9},{2,10},{3,11},{4,12},{5,13},{6,14},{7,15},{8,0},{9,1},... | collective-permute-start | bytes 1859336 | tf_op jit(solution)/shard_map/ppermute | solution.py:390
  83.5 30.7 %collective-permute-start.12 = (bf16[4,144,1076]{2,1,0:T(8,128)(2,1)S(1)}, bf16[4,144,1076]{2,1,0:T(8,128)(2,1)S(1)}, u32[]{:S(2)}, u32[]{:S(2)}) collective-permute-start(bf16[4,144,1076]{2,1,0:T(8,128)(2,1)S(1)} %constant_dynamic-update-slice_fusion.8), channel_id=1, source_target_pairs={{0,4},{1,3},{2,6},{3,1},{4,0},{5,7},{6,2},{7,5},{8,12},{9,11},{10,... | collective-permute-start | bytes 3718664 | tf_op jit(solution)/shard_map/ppermute | solution.py:390
  85.1 28.1 %collective-permute-start.13 = (bf16[2,144,1076]{2,1,0:T(8,128)(2,1)S(1)}, bf16[2,144,1076]{2,1,0:T(8,128)(2,1)S(1)}, u32[]{:S(2)}, u32[]{:S(2)}) collective-permute-start(bf16[2,144,1076]{2,1,0:T(8,128)(2,1)S(1)} %constant_dynamic-update-slice_fusion.10), channel_id=1, source_target_pairs={{0,16},{1,17},{2,18},{3,19},{4,20},{5,21},{6,22},{7,23},{8,24},{9,... | collective-permute-start | bytes 1859336 | tf_op jit(solution)/shard_map/ppermute | solution.py:390
  87.2 19.3 %collective-permute-start.11 = (bf16[4,144,288]{2,1,0:T(8,128)(2,1)S(1)}, bf16[4,144,288]{2,1,0:T(8,128)(2,1)S(1)}, u32[]{:S(2)}, u32[]{:S(2)}) collective-permute-start(bf16[4,144,288]{2,1,0:T(8,128)(2,1)S(1)} %constant_dynamic-update-slice_fusion.12), channel_id=1, source_target_pairs={{0,4},{1,3},{2,6},{3,1},{4,0},{5,7},{6,2},{7,5},{8,12},{9,11},{10,... | collective-permute-start | bytes 995336 | tf_op jit(solution)/shard_map/ppermute | solution.py:390
  106.6 39.3 %collective-permute-start.15 = (bf16[8,144,288]{2,1,0:T(8,128)(2,1)S(1)}, bf16[8,144,288]{2,1,0:T(8,128)(2,1)S(1)}, u32[]{:S(2)}, u32[]{:S(2)}) collective-permute-start(bf16[8,144,288]{2,1,0:T(8,128)(2,1)S(1)} %constant_dynamic-update-slice_fusion.14.refs_0_), channel_id=1, source_target_pairs={{0,2},{1,5},{2,0},{3,7},{4,6},{5,1},{6,4},{7,3},{8,10},{9,13},{10,... | collective-permute-start | bytes 1990664 | tf_op jit(solution)/shard_map/ppermute | solution.py:390
  113.4 30.1 %collective-permute-start.14 = (bf16[4,144,1076]{2,1,0:T(8,128)(2,1)S(1)}, bf16[4,144,1076]{2,1,0:T(8,128)(2,1)S(1)}, u32[]{:S(2)}, u32[]{:S(2)}) collective-permute-start(bf16[4,144,1076]{2,1,0:T(8,128)(2,1)S(1)} %constant_dynamic-update-slice_fusion.18), channel_id=1, source_target_pairs={{0,8},{1,9},{2,10},{3,11},{4,12},{5,13},{6,14},{7,15},{8,0},{9,1},... | collective-permute-start | bytes 3718664 | tf_op jit(solution)/shard_map/ppermute | solution.py:390
  116.6 39.8 %collective-permute-start.17 = (bf16[8,144,1076]{2,1,0:T(8,128)(2,1)}, bf16[8,144,1076]{2,1,0:T(8,128)(2,1)}, u32[]{:S(2)}, u32[]{:S(2)}) collective-permute-start(bf16[8,144,1076]{2,1,0:T(8,128)(2,1)} %constant_dynamic-update-slice_fusion.16.refs_2_), channel_id=1, source_target_pairs={{0,2},{1,5},{2,0},{3,7},{4,6},{5,1},{6,4},{7,3},{8,10},{9,13},{10,... | collective-permute-start | bytes 7437320 | tf_op jit(solution)/shard_map/ppermute | solution.py:390
  153.5 39.9 %collective-permute-start.19 = (bf16[8,144,1076]{2,1,0:T(8,128)(2,1)}, bf16[8,144,1076]{2,1,0:T(8,128)(2,1)}, u32[]{:S(2)}, u32[]{:S(2)}) collective-permute-start(bf16[8,144,1076]{2,1,0:T(8,128)(2,1)} %constant_dynamic-update-slice_fusion.20.refs_2_), channel_id=1, source_target_pairs={{0,2},{1,5},{2,0},{3,7},{4,6},{5,1},{6,4},{7,3},{8,10},{9,13},{10,... | collective-permute-start | bytes 7437320 | tf_op jit(solution)/shard_map/ppermute | solution.py:390
  191.5 35.7 %collective-permute-start.20 = (bf16[8,144,1076]{2,1,0:T(8,128)(2,1)}, bf16[8,144,1076]{2,1,0:T(8,128)(2,1)}, u32[]{:S(2)}, u32[]{:S(2)}) collective-permute-start(bf16[8,144,1076]{2,1,0:T(8,128)(2,1)} %get-tuple-element.156), channel_id=1, source_target_pairs={{0,2},{1,5},{2,0},{3,7},{4,6},{5,1},{6,4},{7,3},{8,10},{9,13},{10,... | collective-permute-start | bytes 7437320 | tf_op jit(solution)/shard_map/ppermute | solution.py:390
  230.9 35.8 %collective-permute-start.24 = (bf16[8,144,1076]{2,1,0:T(8,128)(2,1)}, bf16[8,144,1076]{2,1,0:T(8,128)(2,1)}, u32[]{:S(2)}, u32[]{:S(2)}) collective-permute-start(bf16[8,144,1076]{2,1,0:T(8,128)(2,1)} %get-tuple-element.164), channel_id=1, source_target_pairs={{0,2},{1,5},{2,0},{3,7},{4,6},{5,1},{6,4},{7,3},{8,10},{9,13},{10,... | collective-permute-start | bytes 7437320 | tf_op jit(solution)/shard_map/ppermute | solution.py:390
  232.1 34.6 %collective-permute-start.23 = (bf16[4,144,1076]{2,1,0:T(8,128)(2,1)S(1)}, bf16[4,144,1076]{2,1,0:T(8,128)(2,1)S(1)}, u32[]{:S(2)}, u32[]{:S(2)}) collective-permute-start(bf16[4,144,1076]{2,1,0:T(8,128)(2,1)S(1)} %get-tuple-element.235), channel_id=1, source_target_pairs={{0,8},{1,9},{2,10},{3,11},{4,12},{5,13},{6,14},{7,15},{8,0},{9,1},... | collective-permute-start | bytes 3718664 | tf_op jit(solution)/shard_map/ppermute | solution.py:390
  248.5 28.7 %collective-permute-start.25 = (bf16[8,144,288]{2,1,0:T(8,128)(2,1)S(1)}, bf16[8,144,288]{2,1,0:T(8,128)(2,1)}, u32[]{:S(2)}, u32[]{:S(2)}) collective-permute-start(bf16[8,144,288]{2,1,0:T(8,128)(2,1)S(1)} %get-tuple-element.172), channel_id=1, source_target_pairs={{0,2},{1,5},{2,0},{3,7},{4,6},{5,1},{6,4},{7,3},{8,10},{9,13},{10,... | collective-permute-start | bytes 1990664 | tf_op jit(solution)/shard_map/ppermute | solution.py:390
  271.0 36.4 %collective-permute-start.26 = (bf16[4,144,1076]{2,1,0:T(8,128)(2,1)}, bf16[4,144,1076]{2,1,0:T(8,128)(2,1)S(1)}, u32[]{:S(2)}, u32[]{:S(2)}) collective-permute-start(bf16[4,144,1076]{2,1,0:T(8,128)(2,1)} %get-tuple-element.233), channel_id=1, source_target_pairs={{0,4},{1,3},{2,6},{3,1},{4,0},{5,7},{6,2},{7,5},{8,12},{9,11},{10,... | collective-permute-start | bytes 3718664 | tf_op jit(solution)/shard_map/ppermute | solution.py:390
  273.1 32.3 %collective-permute-start.28 = (bf16[2,144,1076]{2,1,0:T(8,128)(2,1)S(1)}, bf16[2,144,1076]{2,1,0:T(8,128)(2,1)S(1)}, u32[]{:S(2)}, u32[]{:S(2)}) collective-permute-start(bf16[2,144,1076]{2,1,0:T(8,128)(2,1)S(1)} %get-tuple-element.241), channel_id=1, source_target_pairs={{0,16},{1,17},{2,18},{3,19},{4,20},{5,21},{6,22},{7,23},{8,24},{9,... | collective-permute-start | bytes 1859336 | tf_op jit(solution)/shard_map/ppermute | solution.py:390
  278.6 28.3 %collective-permute-start.27 = (bf16[4,144,288]{2,1,0:T(8,128)(2,1)S(1)}, bf16[4,144,288]{2,1,0:T(8,128)(2,1)S(1)}, u32[]{:S(2)}, u32[]{:S(2)}) collective-permute-start(bf16[4,144,288]{2,1,0:T(8,128)(2,1)S(1)} %get-tuple-element.245), channel_id=1, source_target_pairs={{0,4},{1,3},{2,6},{3,1},{4,0},{5,7},{6,2},{7,5},{8,12},{9,11},{10,... | collective-permute-start | bytes 995336 | tf_op jit(solution)/shard_map/ppermute | solution.py:390
  302.2 35.5 %collective-permute-start.33 = (bf16[8,144,864]{2,1,0:T(8,128)(2,1)}, bf16[8,144,864]{2,1,0:T(8,128)(2,1)S(1)}, u32[]{:S(2)}, u32[]{:S(2)}) collective-permute-start(bf16[8,144,864]{2,1,0:T(8,128)(2,1)} %get-tuple-element.186), channel_id=1, source_target_pairs={{0,2},{1,5},{2,0},{3,7},{4,6},{5,1},{6,4},{7,3},{8,10},{9,13},{10,... | collective-permute-start | bytes 5971976 | tf_op jit(solution)/shard_map/ppermute | solution.py:390
  307.0 18.3 %collective-permute-start.32 = (bf16[2,144,288]{2,1,0:T(8,128)(2,1)S(1)}, bf16[2,144,288]{2,1,0:T(8,128)(2,1)S(1)}, u32[]{:S(2)}, u32[]{:S(2)}) collective-permute-start(bf16[2,144,288]{2,1,0:T(8,128)(2,1)S(1)} %get-tuple-element.249), channel_id=1, source_target_pairs={{0,8},{1,9},{2,10},{3,11},{4,12},{5,13},{6,14},{7,15},{8,0},{9,1},... | collective-permute-start | bytes 497672 | tf_op jit(solution)/shard_map/ppermute | solution.py:390
  314.5 18.7 %collective-permute-start.31 = (bf16[2,144,1076]{2,1,0:T(8,128)(2,1)S(1)}, bf16[2,144,1076]{2,1,0:T(8,128)(2,1)S(1)}, u32[]{:S(2)}, u32[]{:S(2)}) collective-permute-start(bf16[2,144,1076]{2,1,0:T(8,128)(2,1)S(1)} %get-tuple-element.239), channel_id=1, source_target_pairs={{0,8},{1,9},{2,10},{3,11},{4,12},{5,13},{6,14},{7,15},{8,0},{9,1},... | collective-permute-start | bytes 1859336 | tf_op jit(solution)/shard_map/ppermute | solution.py:390
  315.6 20.0 %collective-permute-start.30 = (bf16[512,1152]{1,0:T(8,128)(2,1)S(1)}, bf16[512,1152]{1,0:T(8,128)(2,1)S(1)}, u32[]{:S(2)}, u32[]{:S(2)}) collective-permute-start(bf16[512,1152]{1,0:T(8,128)(2,1)S(1)} %slice.411), channel_id=1, source_target_pairs={{0,1},{1,0},{2,3},{3,2},{4,5},{5,4},{6,7},{7,6},{8,9},{9,8},{10,11... | collective-permute-start | bytes 3538952 | tf_op jit(solution)/shard_map/ppermute | solution.py:390
  325.3 22.1 %collective-permute-start.39 = (bf16[1,144,288]{2,1,0:T(8,128)(2,1)S(1)}, bf16[1,144,288]{2,1,0:T(8,128)(2,1)}, u32[]{:S(2)}, u32[]{:S(2)}) collective-permute-start(bf16[1,144,288]{2,1,0:T(8,128)(2,1)S(1)} %add_convert_fusion.25), channel_id=1, source_target_pairs={{0,16},{1,17},{2,18},{3,19},{4,20},{5,21},{6,22},{7,23},{8,24},{9,... | collective-permute-start | bytes 248840 | tf_op jit(solution)/shard_map/ppermute | solution.py:390
  334.2 20.6 %collective-permute-start.38 = (bf16[1,144,1076]{2,1,0:T(8,128)(2,1)}, bf16[1,144,1076]{2,1,0:T(8,128)(2,1)S(1)}, u32[]{:S(2)}, u32[]{:S(2)}) collective-permute-start(bf16[1,144,1076]{2,1,0:T(8,128)(2,1)} %add_convert_fusion.18), channel_id=1, source_target_pairs={{0,16},{1,17},{2,18},{3,19},{4,20},{5,21},{6,22},{7,23},{8,24},{9,... | collective-permute-start | bytes 929672 | tf_op jit(solution)/shard_map/ppermute | solution.py:390
  340.1 17.5 %collective-permute-start.37 = (bf16[4,144,864]{2,1,0:T(8,128)(2,1)}, bf16[4,144,864]{2,1,0:T(8,128)(2,1)}, u32[]{:S(2)}, u32[]{:S(2)}) collective-permute-start(bf16[4,144,864]{2,1,0:T(8,128)(2,1)} %get-tuple-element.237), channel_id=1, source_target_pairs={{0,4},{1,3},{2,6},{3,1},{4,0},{5,7},{6,2},{7,5},{8,12},{9,11},{10,... | collective-permute-start | bytes 2985992 | tf_op jit(solution)/shard_map/ppermute | solution.py:390
  344.3 20.6 %collective-permute-start.44 = (bf16[1,144,1076]{2,1,0:T(8,128)(2,1)}, bf16[1,144,1076]{2,1,0:T(8,128)(2,1)S(1)}, u32[]{:S(2)}, u32[]{:S(2)}) collective-permute-start(bf16[1,144,1076]{2,1,0:T(8,128)(2,1)} %add_convert_fusion.19), channel_id=1, source_target_pairs={{0,4},{1,3},{2,6},{3,1},{4,0},{5,7},{6,2},{7,5},{8,12},{9,11},{10,... | collective-permute-start | bytes 929672 | tf_op jit(solution)/shard_map/ppermute | solution.py:390
  347.3 27.2 %collective-permute-start.29 = (bf16[512,1152]{1,0:T(8,128)(2,1)S(1)}, bf16[512,1152]{1,0:T(8,128)(2,1)S(1)}, u32[]{:S(2)}, u32[]{:S(2)}) collective-permute-start(bf16[512,1152]{1,0:T(8,128)(2,1)S(1)} %slice.412), channel_id=1, source_target_pairs={{0,1},{1,0},{2,3},{3,2},{4,5},{5,4},{6,7},{7,6},{8,9},{9,8},{10,11... | collective-permute-start | bytes 3538952 | tf_op jit(solution)/shard_map/ppermute | solution.py:390
  373.3 12.6 %collective-permute-start.43 = (bf16[1,144,864]{2,1,0:T(8,128)(2,1)S(1)}, bf16[1,144,864]{2,1,0:T(8,128)(2,1)S(1)}, u32[]{:S(2)}, u32[]{:S(2)}) collective-permute-start(bf16[1,144,864]{2,1,0:T(8,128)(2,1)S(1)} %add_convert_fusion.21), channel_id=1, source_target_pairs={{0,16},{1,17},{2,18},{3,19},{4,20},{5,21},{6,22},{7,23},{8,24},{9,... | collective-permute-start | bytes 746504 | tf_op jit(solution)/shard_map/ppermute | solution.py:390
  (101 other events, 1187.0 us)
where the time goes:
time: 391 us; the launch traced here: 387 us
  Pallas kernels  128 us (33%)
  waiting for transfers between devices  112 us (29%)
  starting transfers between devices  57.4 us (15%)
  other arithmetic  36.8 us (9%)
  matrix products  25.7 us (7%)
  local copies, waits for them, and re-layouts  24.8 us (6%)
    ppermute x45, waiting for transfers between devices, permute(): return lax.ppermute(values, ('dp', 'tensor'), pairs)  112 us
    ppermute x45, starting transfers between devices, permute(): return lax.ppermute(values, ('dp', 'tensor'), pairs)  57.4 us
    pallas_call x4, Pallas kernels, weight_grad(): pl.pallas_call(functools.partial(weight_grad_body, images, n_dp, half), i...  36.8 us
    pallas_call x2, Pallas kernels, attend_backward(): pl.pallas_call(functools.partial(attend_backward_body, heads), in_specs=[...  29.4 us
    dot_general x8, matrix products, dot(): return lax.dot_general(left, right, dims, preferred_element_type=F32)  25.7 us
    pallas_call x2, Pallas kernels, attend_forward(): kernel_call(functools.partial(attend_forward_body, heads, len(parts)), 'a...  23 us
    pallas_call x2, Pallas kernels, up(): kernel_call(functools.partial(up_body, len(parts)), 'up', 1, len(parts),...  19.2 us
    pallas_call x2, Pallas kernels, pre_grad(): kernel_call(functools.partial(pre_grad_body, len(parts)), 'pre_grad', 0,...  15.3 us
  transfers between devices with their start and end apart: 45, of which 22 were waited for; matrix products, arithmetic and copies ran while one was open for 18% of the time, Pallas kernels for 33%

commit v1 on v0

--- a/solution.py
+++ b/solution.py
@@ -430,15 +430,17 @@
 
 
 class Gather:
-    def __init__(self, plan, order, shard, way="far"):
+    def __init__(self, plan, order, shard, way="far", joined=True):
         self.plan, self.order, self.held, self.stage, self.way = plan, order, (shard[None],), 0, way
+        self.joined = joined
 
     def to(self, stage, *after):
         while self.stage < stage:
             held = tie(self.held, [*self.order.done, *after])
-            mine = held[0] if len(held) == 1 else jnp.concatenate(held, axis=0)
-            self.held = (mine, self.plan.exchange(mine, self.stage, self.way))
-            self.order.begun.append(mine)
+            if len(held) > 1 and (self.joined or self.stage < self.plan.stages - 1):
+                held = (jnp.concatenate(held, axis=0),)
+            self.held = (*held, *(self.plan.exchange(mine, self.stage, self.way) for mine in held))
+            self.order.begun.append(held[0])
             self.stage += 1
         return self.held[-1]
 
@@ -466,8 +468,9 @@
             self.order.begun.append(self.send)
         return self.theirs
 
-    def finish(self):
+    def finish(self, *after):
         self.to(0)
+        self.keep, self.theirs = tie((self.keep, self.theirs), after)
         return self.total(0)
 
 
@@ -516,7 +519,7 @@
     gather_qkv = Gather(plan, order, jnp.concatenate([low(w_query), low(w_key), low(w_value)], axis=1))
     gather_out = Gather(plan, order, low(w_out).T)
     gather_up = Gather(plan, order, low(w_up))
-    gather_down = Gather(plan, order, low(w_down).T, "near")
+    gather_down = Gather(plan, order, low(w_down).T, "near", joined=False)
     cot_rows = plan.rank_gather(cotangent)
     inputs32 = tokens.astype(F32)
     normed_one = low(layer_norm(inputs32, gain_one, shift_one))
@@ -548,13 +551,13 @@
             gather_out.to(last)
             gather_up.to(last)
             gather_down.to(near)
+
+    out_full = [placed(gather_out.weight(), order.enter, i, "place_out") for i in each]
+    attn = sum(dot(mixed[i], out_full[i], NT) for i in each)
+    order.leave(attn[:8])
     gather_down.to(last)
-
-    out_full = [placed(gather_out.weight(), order.enter, i, "place_out") for i in each]
-    down_held = [] if gather_down.stage < last else [gather_down.held[0]]
-    attn = sum(dot(mixed[i], out_full[i], NT) for i in each)
-    (attn,) = tie((attn,), down_held)
-    residual = inputs32 + plan.rank_scatter(attn, gather_up.held[-1]) + b_out
+    (attn,) = tie((order.enter(attn),), [gather_up.held[-1]])
+    residual = inputs32 + plan.rank_scatter(attn) + b_out
     normed_two = low(layer_norm(residual, gain_two, shift_two))
     order.leave(normed_two[:8])
     rows_two = plan.rank_gather(normed_two)
@@ -603,21 +606,24 @@
     scatter_down.to(0)
     partial_one = sum(dot(order.enter(qkv_grads[i]), qkv_full[i], NT) for i in each)
     order.leave(partial_one[:8])
+    down_grad = scatter_down.finish(*order.done)
+    order.begun.append(down_grad)
     mlp = sum(dot(order.enter(act[i]), down_full[i], NT) for i in each)
     order.leave(mlp[:8])
     scatter_up.to(0)
     scatter_out.to(0)
-    norm_one_grad = order.enter(plan.rank_scatter(partial_one))
+    mlp = plan.rank_scatter(mlp)
+    (norm_one_grad,) = tie((order.enter(plan.rank_scatter(partial_one)),), [mlp])
     _, pull_one = jax.vjp(layer_norm, inputs32, gain_one, shift_one)
     input_part, gain_one_grad, shift_one_grad = pull_one(norm_one_grad)
     grad_tokens = low(residual_grad + input_part)
-    output = low(residual + plan.rank_scatter(mlp) + b_down)
+    output = low(residual + mlp + b_down)
     order.leave(gain_one_grad)
     scatter_qkv.to(far)
-    gain_one_grad = order.enter(gain_one_grad)
-    down_grad = scatter_down.finish().T
     up_grad = scatter_up.finish()
     out_grad = scatter_out.finish().T
+    down_grad = down_grad.T
+    gain_one_grad = order.enter(gain_one_grad)
     qkv_sums = [jnp.sum(grads, axis=0, dtype=F32) for grads in qkv_grads]
     up_bias_grad = uncolumns([order.enter(part)[0] for part in up_bias_parts], b_up.shape[0])
     query_bias_grad = uncolumns([sums[:head_cols] for sums in qkv_sums], b_query.shape[0])
@@ -633,9 +639,9 @@
         together = together + plan.rank_exchange(together, stage)
     for stage in range(plan.stages):
         together = together + plan.exchange(together, stage)
-        if stage in (first, near):
+        if stage in (first - 1, first):
             order.leave(together)
-            if stage == first:
+            if stage == first - 1:
                 scatter_qkv.to(first, up_grad, out_grad)
             else:
                 scatter_qkv.to(0)

time: 391 us -> 385 us (0.985)
  waiting for transfers between devices: 112 us -> 118 us
  local copies, waits for them, and re-layouts: 24.8 us -> 19.9 us
    ppermute x45 -> x46, waiting for transfers between devices: 112 us -> 118 us  [permute(): return lax.ppermute(values, ('dp', 'tensor'), pairs)]
    ppermute x45 -> x46, starting transfers between devices: 57.4 us -> 54.5 us  [permute(): return lax.ppermute(values, ('dp', 'tensor'), pairs)]
    unnamed x187 -> x184, local copies, waits for them, and re-layouts: 13.6 us -> 12.1 us
    convert_element_type x8 -> x9, other arithmetic: 13.5 us -> 13.5 us  [to(): self.total(slice(half)).astype(LOW)]
  transfers between devices with their start and end apart: 45 -> 46, of which waited for: 22 -> 26; matrix products, arithmetic and copies ran while one was open for 18% -> 15% of each run, Pallas kernels for 33% -> 34%
where the time goes in v1:
time: 385 us; the launch traced here: 381 us
  Pallas kernels  128 us (33%)
  waiting for transfers between devices  118 us (31%)
  starting transfers between devices  54.5 us (14%)
  other arithmetic  35 us (9%)
  matrix products  23.7 us (6%)
  local copies, waits for them, and re-layouts  19.9 us (5%)
    ppermute x46, waiting for transfers between devices, permute(): return lax.ppermute(values, ('dp', 'tensor'), pairs)  118 us
    ppermute x46, starting transfers between devices, permute(): return lax.ppermute(values, ('dp', 'tensor'), pairs)  54.5 us
    pallas_call x4, Pallas kernels, weight_grad(): pl.pallas_call(functools.partial(weight_grad_body, images, n_dp, half), i...  36.6 us
    pallas_call x2, Pallas kernels, attend_backward(): pl.pallas_call(functools.partial(attend_backward_body, heads), in_specs=[...  29.3 us
    dot_general x8, matrix products, dot(): return lax.dot_general(left, right, dims, preferred_element_type=F32)  23.7 us
    pallas_call x2, Pallas kernels, attend_forward(): kernel_call(functools.partial(attend_forward_body, heads, len(parts)), 'a...  23 us
    pallas_call x2, Pallas kernels, up(): kernel_call(functools.partial(up_body, len(parts)), 'up', 1, len(parts),...  19.1 us
    pallas_call x2, Pallas kernels, pre_grad(): kernel_call(functools.partial(pre_grad_body, len(parts)), 'pre_grad', 0,...  15.3 us
  transfers between devices with their start and end apart: 46, of which 26 were waited for; matrix products, arithmetic and copies ran while one was open for 15% of the time, Pallas kernels for 34%

profile of v1, /device:TPU:0, one launch (start us, length us, event | category | flops | bytes accessed | tf_op | source)
XLA Modules:
  0.0 380.8 jit_solution(12450311790630955257)
XLA Ops:
  3.8 4.1 %collective-permute-start = (bf16[1,144,864]{2,1,0:T(8,128)(2,1)S(1)}, bf16[1,144,864]{2,1,0:T(8,128)(2,1)S(1)}, u32[]{:S(2)}, u32[]{:S(2)}) collective-permute-start(bf16[1,144,864]{2,1,0:T(8,128)(2,1)S(1)} %maximum_bitcast_fusion), channel_id=1, source_target_pairs={{0,16},{1,17},{2,18},{3,19},{4,20},{5,21},{6,22},{7,23},{8,24},{9,... | collective-permute-start | bytes 746504 | tf_op jit(solution)/shard_map/ppermute | solution.py:390
  10.3 9.3 %collective-permute-done = bf16[1,144,864]{2,1,0:T(8,128)(2,1)S(1)} collective-permute-done((bf16[1,144,864]{2,1,0:T(8,128)(2,1)S(1)}, bf16[1,144,864]{2,1,0:T(8,128)(2,1)S(1)}, u32[]{:S(2)}, u32[]{:S(2)}) %collective-permute-start) | collective-permute-done | bytes 248864 | tf_op jit(solution)/shard_map/ppermute | solution.py:390
  22.2 3.4 collective-permute-start.3
  27.8 6.3 %collective-permute-done.3 = bf16[1,144,288]{2,1,0:T(8,128)(2,1)S(1)} collective-permute-done((bf16[1,144,288]{2,1,0:T(8,128)(2,1)S(1)}, bf16[1,144,288]{2,1,0:T(8,128)(2,1)S(1)}, u32[]{:S(2)}, u32[]{:S(2)}) %collective-permute-start.3) | collective-permute-done | bytes 82976 | tf_op jit(solution)/shard_map/ppermute | solution.py:390
  43.5 8.3 %collective-permute-done.9 = bf16[2,144,288]{2,1,0:T(8,128)(2,1)S(1)} collective-permute-done((bf16[2,144,288]{2,1,0:T(8,128)(2,1)S(1)}, bf16[2,144,288]{2,1,0:T(8,128)(2,1)S(1)}, u32[]{:S(2)}, u32[]{:S(2)}) %collective-permute-start.9) | collective-permute-done | bytes 165920 | tf_op jit(solution)/shard_map/ppermute | solution.py:390
  51.9 3.1 collective-permute-done.2
  62.1 15.1 %collective-permute-done.8 = bf16[2,144,1076]{2,1,0:T(8,128)(2,1)S(1)} collective-permute-done((bf16[2,144,1076]{2,1,0:T(8,128)(2,1)S(1)}, bf16[2,144,1076]{2,1,0:T(8,128)(2,1)S(1)}, u32[]{:S(2)}, u32[]{:S(2)}) %collective-permute-start.8) | collective-permute-done | bytes 619808 | tf_op jit(solution)/shard_map/ppermute | solution.py:390
  77.2 6.6 %collective-permute-done.10.refs_3_ = bf16[8,144,864]{2,1,0:T(8,128)(2,1)} collective-permute-done((bf16[8,144,864]{2,1,0:T(8,128)(2,1)}, bf16[8,144,864]{2,1,0:T(8,128)(2,1)}, u32[]{:S(2)}, u32[]{:S(2)}) %collective-permute-start.10) | collective-permute-done | bytes 1990688 | tf_op jit(solution)/shard_map/ppermute | solution.py:390
  88.4 11.5 %attend_forward.2 = (bf16[1024,864]{1,0:T(8,128)(2,1)}, bf16[1024,288]{1,0:T(8,128)(2,1)S(1)}, f32[4,1024]{1,0:T(4,128)S(1)}, bf16[1152,864]{1,0:T(8,128)(2,1)}) custom-call(s32[8]{0:T(128)S(1)} %get-tuple-element.148.table_ref, f32[1,864]{1,0:T(1,128)S(1)} %broadcast_in_dim.276.bias_ref, bf16[512,1152]{1,0:T(8,128)(2,1)S(1)} %fusion.7.refs_0_, ...), custom_call_target="tpu_custom_call" | custom-call | flops 8480882688 | bytes 6356992 | tf_op jit(solution)/shard_map/attend_forward/pallas_call | solution.py:161
  103.1 8.4 %collective-permute-done.11 = bf16[4,144,288]{2,1,0:T(8,128)(2,1)S(1)} collective-permute-done((bf16[4,144,288]{2,1,0:T(8,128)(2,1)S(1)}, bf16[4,144,288]{2,1,0:T(8,128)(2,1)S(1)}, u32[]{:S(2)}, u32[]{:S(2)}) %collective-permute-start.11) | collective-permute-done | bytes 331808 | tf_op jit(solution)/shard_map/ppermute | solution.py:390
  116.4 11.5 %attend_forward.3 = (bf16[1024,864]{1,0:T(8,128)(2,1)}, bf16[1024,288]{1,0:T(8,128)(2,1)S(1)}, f32[4,1024]{1,0:T(4,128)S(1)}, bf16[1152,864]{1,0:T(8,128)(2,1)}) custom-call(s32[8]{0:T(128)S(1)} %get-tuple-element.150.table_ref, f32[1,864]{1,0:T(1,128)S(1)} %broadcast_in_dim.281.bias_ref, bf16[512,1152]{1,0:T(8,128)(2,1)S(1)} %fusion.7.refs_0_, ...), custom_call_target="tpu_custom_call" | custom-call | flops 8480882688 | bytes 6356992 | tf_op jit(solution)/shard_map/attend_forward/pallas_call | solution.py:161
  127.9 16.0 %collective-permute-done.14.refs_1_ = bf16[8,144,288]{2,1,0:T(8,128)(2,1)S(1)} collective-permute-done((bf16[8,144,288]{2,1,0:T(8,128)(2,1)S(1)}, bf16[8,144,288]{2,1,0:T(8,128)(2,1)S(1)}, u32[]{:S(2)}, u32[]{:S(2)}) %collective-permute-start.14) | collective-permute-done | bytes 663584 | tf_op jit(solution)/shard_map/ppermute | solution.py:390
  160.8 9.3 %up.2 = (bf16[1024,1076]{1,0:T(8,128)(2,1)}, bf16[1024,1076]{1,0:T(8,128)(2,1)}, bf16[1152,1076]{1,0:T(8,128)(2,1)}) custom-call(s32[8]{0:T(128)S(1)} %copy-done.21, f32[1,1076]{1,0:T(1,128)S(1)} %broadcast_in_dim.282.bias_ref, bf16[512,1152]{1,0:T(8,128)(2,1)} %add_convert_fusion.6.refs_0_, bf16[512,1152]{1,0:T(8,128)(2,1)} %collective-permute-done.18.refs_1_, ...), custom_call_target="tpu_custom_call" | custom-call | flops 2538602496 | bytes 9365504 | tf_op jit(solution)/shard_map/up/pallas_call | solution.py:221
  170.2 9.8 %up.3 = (bf16[1024,1076]{1,0:T(8,128)(2,1)}, bf16[1024,1076]{1,0:T(8,128)(2,1)}, bf16[1152,1076]{1,0:T(8,128)(2,1)}) custom-call(s32[8]{0:T(128)S(1)} %copy-done.19, f32[1,1076]{1,0:T(1,128)S(1)} %broadcast_in_dim.283.bias_ref, bf16[512,1152]{1,0:T(8,128)(2,1)} %add_convert_fusion.6.refs_0_, bf16[512,1152]{1,0:T(8,128)(2,1)} %collective-permute-done.18.refs_1_, ...), custom_call_target="tpu_custom_call" | custom-call | flops 2538602496 | bytes 9365504 | tf_op jit(solution)/shard_map/up/pallas_call | solution.py:221
  180.0 9.9 %grad_down.1 = (bf16[8,144,1076]{2,1,0:T(8,128)(2,1)}, bf16[8,144,1076]{2,1,0:T(8,128)(2,1)}) custom-call(s32[16]{0:T(128)S(1)} %select_n.272.table_ref, bf16[512,1152]{1,0:T(8,128)(2,1)S(1)} %copy-done, bf16[512,1152]{1,0:T(8,128)(2,1)S(1)} %collective-permute-done.6.refs_1_, bf16[1024,1076]{1,0:T(8,128)(2,1)} %get-tuple-element.202.refs_2_, ...), custom_call_target="tpu_custom_call" | custom-call | tf_op jit(solution)/shard_map/grad_down/pallas_call | solution.py:354
  190.6 7.6 %pre_grad.2 = (bf16[1024,1076]{1,0:T(8,128)(2,1)}, f32[1,1076]{1,0:T(1,128)S(1)}, bf16[1152,1076]{1,0:T(8,128)(2,1)}) custom-call(s32[8]{0:T(128)S(1)} %get-tuple-element.159.table_ref, bf16[1024,1076]{1,0:T(8,128)(2,1)} %get-tuple-element.160.slope_in, bf16[512,1152]{1,0:T(8,128)(2,1)S(1)} %copy-done, bf16[512,1152]{1,0:T(8,128)(2,1)S(1)} %collective-permute-done.6.refs_1_, ...), custom_call_target="tpu_custom_call" | custom-call | flops 2538602496 | bytes 7166160 | tf_op jit(solution)/shard_map/pre_grad/pallas_call | solution.py:252
  198.3 7.7 %pre_grad.3 = (bf16[1024,1076]{1,0:T(8,128)(2,1)}, f32[1,1076]{1,0:T(1,128)S(1)}, bf16[1152,1076]{1,0:T(8,128)(2,1)}) custom-call(s32[8]{0:T(128)S(1)} %get-tuple-element.164.table_ref, bf16[1024,1076]{1,0:T(8,128)(2,1)} %get-tuple-element.165.slope_in, bf16[512,1152]{1,0:T(8,128)(2,1)S(1)} %copy-done, bf16[512,1152]{1,0:T(8,128)(2,1)S(1)} %collective-permute-done.6.refs_1_, ...), custom_call_target="tpu_custom_call" | custom-call | flops 2538602496 | bytes 7166160 | tf_op jit(solution)/shard_map/pre_grad/pallas_call | solution.py:252
  206.0 10.8 %grad_up.1 = (bf16[8,144,1076]{2,1,0:T(8,128)(2,1)}, bf16[8,144,1076]{2,1,0:T(8,128)(2,1)}) custom-call(s32[16]{0:T(128)S(1)} %select_n.266.table_ref, bf16[512,1152]{1,0:T(8,128)(2,1)} %add_convert_fusion.6.refs_0_, bf16[512,1152]{1,0:T(8,128)(2,1)} %collective-permute-done.18.refs_1_, bf16[1024,1076]{1,0:T(8,128)(2,1)} %get-tuple-element.162.refs_2_, ...), custom_call_target="tpu_custom_call" | custom-call | tf_op jit(solution)/shard_map/grad_up/pallas_call | solution.py:354
  216.8 3.5 fusion.35
  220.4 4.1 %convolution_add_fusion.3 = f32[1024,1152]{1,0:T(8,128)S(1)} fusion(f32[1024,1152]{1,0:T(8,128)S(1)} %fusion.35, bf16[1024,1076]{1,0:T(8,128)(2,1)S(1)} %copy-done.40, bf16[1152,1076]{1,0:T(8,128)(2,1)S(1)} %copy-done.83), kind=kOutput, calls=%fused_computation.3 | convolution fusion | flops 2539782144 | bytes 14119936 | tf_op jit(solution)/shard_map/dot_general | solution.py:29
  224.5 3.4 add_convert_fusion.2
  238.4 7.4 %grad_out.1 = (bf16[8,144,288]{2,1,0:T(8,128)(2,1)S(1)}, bf16[8,144,288]{2,1,0:T(8,128)(2,1)S(1)}) custom-call(s32[16]{0:T(128)S(1)} %select_n.266.table_ref, bf16[512,1152]{1,0:T(8,128)(2,1)} %copy-done.1, bf16[512,1152]{1,0:T(8,128)(2,1)} %copy-done.3, bf16[1024,288]{1,0:T(8,128)(2,1)S(1)} %copy-done.10, bf16[1024,288]{1,0:T(8,128)(2,1)S(1)} %copy-done.8), custom_call_target="tpu_custom_call" | custom-call | tf_op jit(solution)/shard_map/grad_out/pallas_call | solution.py:354
  249.6 14.8 %attend_backward.2.refs_2_ = bf16[1024,864]{1,0:T(8,128)(2,1)} custom-call(f32[4,1024]{1,0:T(4,128)S(1)} %copy-done.17, bf16[1024,864]{1,0:T(8,128)(2,1)} %get-tuple-element.177.qkv_in, bf16[1024,288]{1,0:T(8,128)(2,1)S(1)} %copy-done.10, bf16[1152,288]{1,0:T(8,128)(2,1)S(1)} %copy-done.6, bf16[512,1152]{1,0:T(8,128)(2,1)S(1)} %copy-done.2, ...), custom_call_target="tpu_custom_call" | custom-call | tf_op jit(solution)/shard_map/attend_backward/pallas_call | solution.py:291
  264.4 4.4 %add_convert_fusion = (bf16[4,144,1076]{2,1,0:T(8,128)(2,1)}, bf16[4,144,1076]{2,1,0:T(8,128)(2,1)}) fusion(bf16[8,144,1076]{2,1,0:T(8,128)(2,1)} %collective-permute-done.25, bf16[8,144,1076]{2,1,0:T(8,128)(2,1)S(1)} %copy-done.36), kind=kLoop, calls=%fused_computation.19 | loop fusion | flops 4958208 | bytes 7437312 | tf_op jit(solution)/shard_map/convert_element_type | solution.py:465
  275.8 14.5 %attend_backward.3.refs_3_ = bf16[1024,864]{1,0:T(8,128)(2,1)} custom-call(f32[4,1024]{1,0:T(4,128)S(1)} %get-tuple-element.186.lse_ref, bf16[1024,864]{1,0:T(8,128)(2,1)} %get-tuple-element.187.qkv_in, bf16[1024,288]{1,0:T(8,128)(2,1)S(1)} %copy-done.8, bf16[1152,288]{1,0:T(8,128)(2,1)S(1)} %place_out.3.out_in, bf16[512,1152]{1,0:T(8,128)(2,1)S(1)} %copy-done.2, ...), custom_call_target="tpu_custom_call" | custom-call | tf_op jit(solution)/shard_map/attend_backward/pallas_call | solution.py:291
  290.3 8.4 %grad_qkv.1 = (bf16[8,144,864]{2,1,0:T(8,128)(2,1)}, bf16[8,144,864]{2,1,0:T(8,128)(2,1)}) custom-call(s32[16]{0:T(128)S(1)} %select_n.266.table_ref, bf16[512,1152]{1,0:T(8,128)(2,1)S(1)} %copy-done.12, bf16[512,1152]{1,0:T(8,128)(2,1)S(1)} %copy-done.15, bf16[1024,864]{1,0:T(8,128)(2,1)} %attend_backward.2.refs_2_, bf16[1024,864]{1,0:T(8,128)(2,1)} %attend_backward.3.refs_3_), custom_call_target="tpu_custom_call" | custom-call | tf_op jit(solution)/shard_map/grad_qkv/pallas_call | solution.py:354
  313.7 3.6 fusion.37
  317.3 3.9 %convolution_add_fusion.2 = f32[1024,1152]{1,0:T(8,128)S(1)} fusion(f32[1024,1152]{1,0:T(8,128)S(1)} %fusion.37, bf16[1024,1076]{1,0:T(8,128)(2,1)S(1)} %copy-done.38, bf16[1152,1076]{1,0:T(8,128)(2,1)S(1)} %copy-done.81), kind=kOutput, calls=%fused_computation.2 | convolution fusion | flops 2539782144 | bytes 14119936 | tf_op jit(solution)/shard_map/dot_general | solution.py:29
  321.9 3.4 collective-permute-start.40
  325.4 5.5 %collective-permute-done.33 = bf16[2,144,1076]{2,1,0:T(8,128)(2,1)S(1)} collective-permute-done((bf16[2,144,1076]{2,1,0:T(8,128)(2,1)S(1)}, bf16[2,144,1076]{2,1,0:T(8,128)(2,1)S(1)}, u32[]{:S(2)}, u32[]{:S(2)}) %collective-permute-start.33) | collective-permute-done | bytes 619808 | tf_op jit(solution)/shard_map/ppermute | solution.py:390
  350.4 4.2 %collective-permute-done.38 = bf16[4,144,864]{2,1,0:T(8,128)(2,1)S(1)} collective-permute-done((bf16[4,144,864]{2,1,0:T(8,128)(2,1)}, bf16[4,144,864]{2,1,0:T(8,128)(2,1)S(1)}, u32[]{:S(2)}, u32[]{:S(2)}) %collective-permute-start.38) | collective-permute-done | bytes 995360 | tf_op jit(solution)/shard_map/ppermute | solution.py:390
  357.3 10.2 %collective-permute-done.41 = f32[14336]{0:T(1024)S(1)} collective-permute-done((f32[14336]{0:T(1024)S(1)}, f32[14336]{0:T(1024)S(1)}, u32[]{:S(2)}, u32[]{:S(2)}) %collective-permute-start.41) | collective-permute-done | bytes 57376 | tf_op jit(solution)/shard_map/ppermute | solution.py:390
  (366 shorter events, 128.4 us)
Async XLA Ops:
  3.8 15.8 %collective-permute-start = (bf16[1,144,864]{2,1,0:T(8,128)(2,1)S(1)}, bf16[1,144,864]{2,1,0:T(8,128)(2,1)S(1)}, u32[]{:S(2)}, u32[]{:S(2)}) collective-permute-start(bf16[1,144,864]{2,1,0:T(8,128)(2,1)S(1)} %maximum_bitcast_fusion), channel_id=1, source_target_pairs={{0,16},{1,17},{2,18},{3,19},{4,20},{5,21},{6,22},{7,23},{8,24},{9,... | collective-permute-start | bytes 746504 | tf_op jit(solution)/shard_map/ppermute | solution.py:390
  9.8 25.3 %collective-permute-start.5 = (bf16[512,1152]{1,0:T(8,128)(2,1)S(1)}, bf16[512,1152]{1,0:T(8,128)(2,1)S(1)}, u32[]{:S(2)}, u32[]{:S(2)}) collective-permute-start(bf16[512,1152]{1,0:T(8,128)(2,1)S(1)} %fusion.7.refs_0_), channel_id=1, source_target_pairs={{0,1},{1,0},{2,3},{3,2},{4,5},{5,4},{6,7},{7,6},{8,9},{9,8},{10,11... | collective-permute-start | bytes 3538952 | tf_op jit(solution)/shard_map/ppermute | solution.py:390
  9.9 26.3 %collective-permute-start.6 = (bf16[512,1152]{1,0:T(8,128)(2,1)S(1)}, bf16[512,1152]{1,0:T(8,128)(2,1)S(1)}, u32[]{:S(2)}, u32[]{:S(2)}) collective-permute-start(bf16[512,1152]{1,0:T(8,128)(2,1)S(1)} %copy-done), channel_id=1, source_target_pairs={{0,1},{1,0},{2,3},{3,2},{4,5},{5,4},{6,7},{7,6},{8,9},{9,8},{10,11... | collective-permute-start | bytes 3538952 | tf_op jit(solution)/shard_map/ppermute | solution.py:390
  19.7 15.4 %collective-permute-start.1 = (bf16[2,144,864]{2,1,0:T(8,128)(2,1)S(1)}, bf16[2,144,864]{2,1,0:T(8,128)(2,1)S(1)}, u32[]{:S(2)}, u32[]{:S(2)}) collective-permute-start(bf16[2,144,864]{2,1,0:T(8,128)(2,1)S(1)} %pad_maximum_fusion), channel_id=1, source_target_pairs={{0,8},{1,9},{2,10},{3,11},{4,12},{5,13},{6,14},{7,15},{8,0},{9,1},... | collective-permute-start | bytes 1493000 | tf_op jit(solution)/shard_map/ppermute | solution.py:390
  36.3 19.4 %collective-permute-start.7 = (bf16[4,144,864]{2,1,0:T(8,128)(2,1)S(1)}, bf16[4,144,864]{2,1,0:T(8,128)(2,1)S(1)}, u32[]{:S(2)}, u32[]{:S(2)}) collective-permute-start(bf16[4,144,864]{2,1,0:T(8,128)(2,1)S(1)} %constant_dynamic-update-slice_fusion), channel_id=1, source_target_pairs={{0,4},{1,3},{2,6},{3,1},{4,0},{5,7},{6,2},{7,5},{8,12},{9,11},{10,... | collective-permute-start | bytes 2985992 | tf_op jit(solution)/shard_map/ppermute | solution.py:390
  38.3 16.6 %collective-permute-start.2 = (bf16[1,144,1076]{2,1,0:T(8,128)(2,1)S(1)}, bf16[1,144,1076]{2,1,0:T(8,128)(2,1)S(1)}, u32[]{:S(2)}, u32[]{:S(2)}) collective-permute-start(bf16[1,144,1076]{2,1,0:T(8,128)(2,1)S(1)} %convert_bitcast_fusion.1), channel_id=1, source_target_pairs={{0,16},{1,17},{2,18},{3,19},{4,20},{5,21},{6,22},{7,23},{8,24},{9,... | collective-permute-start | bytes 929672 | tf_op jit(solution)/shard_map/ppermute | solution.py:390
  57.8 26.0 %collective-permute-start.10 = (bf16[8,144,864]{2,1,0:T(8,128)(2,1)}, bf16[8,144,864]{2,1,0:T(8,128)(2,1)}, u32[]{:S(2)}, u32[]{:S(2)}) collective-permute-start(bf16[8,144,864]{2,1,0:T(8,128)(2,1)} %constant_dynamic-update-slice_fusion.6.refs_2_), channel_id=1, source_target_pairs={{0,2},{1,5},{2,0},{3,7},{4,6},{5,1},{6,4},{7,3},{8,10},{9,13},{10,... | collective-permute-start | bytes 5971976 | tf_op jit(solution)/shard_map/ppermute | solution.py:390
  60.6 16.6 %collective-permute-start.8 = (bf16[2,144,1076]{2,1,0:T(8,128)(2,1)S(1)}, bf16[2,144,1076]{2,1,0:T(8,128)(2,1)S(1)}, u32[]{:S(2)}, u32[]{:S(2)}) collective-permute-start(bf16[2,144,1076]{2,1,0:T(8,128)(2,1)S(1)} %constant_dynamic-update-slice_fusion.2), channel_id=1, source_target_pairs={{0,8},{1,9},{2,10},{3,11},{4,12},{5,13},{6,14},{7,15},{8,0},{9,1},... | collective-permute-start | bytes 1859336 | tf_op jit(solution)/shard_map/ppermute | solution.py:390
  84.0 18.1 %collective-permute-start.12 = (bf16[4,144,1076]{2,1,0:T(8,128)(2,1)S(1)}, bf16[4,144,1076]{2,1,0:T(8,128)(2,1)S(1)}, u32[]{:S(2)}, u32[]{:S(2)}) collective-permute-start(bf16[4,144,1076]{2,1,0:T(8,128)(2,1)S(1)} %constant_dynamic-update-slice_fusion.8), channel_id=1, source_target_pairs={{0,4},{1,3},{2,6},{3,1},{4,0},{5,7},{6,2},{7,5},{8,12},{9,11},{10,... | collective-permute-start | bytes 3718664 | tf_op jit(solution)/shard_map/ppermute | solution.py:390
  85.6 28.2 %collective-permute-start.13 = (bf16[2,144,1076]{2,1,0:T(8,128)(2,1)S(1)}, bf16[2,144,1076]{2,1,0:T(8,128)(2,1)S(1)}, u32[]{:S(2)}, u32[]{:S(2)}) collective-permute-start(bf16[2,144,1076]{2,1,0:T(8,128)(2,1)S(1)} %constant_dynamic-update-slice_fusion.10), channel_id=1, source_target_pairs={{0,16},{1,17},{2,18},{3,19},{4,20},{5,21},{6,22},{7,23},{8,24},{9,... | collective-permute-start | bytes 1859336 | tf_op jit(solution)/shard_map/ppermute | solution.py:390
  87.8 23.7 %collective-permute-start.11 = (bf16[4,144,288]{2,1,0:T(8,128)(2,1)S(1)}, bf16[4,144,288]{2,1,0:T(8,128)(2,1)S(1)}, u32[]{:S(2)}, u32[]{:S(2)}) collective-permute-start(bf16[4,144,288]{2,1,0:T(8,128)(2,1)S(1)} %constant_dynamic-update-slice_fusion.12), channel_id=1, source_target_pairs={{0,4},{1,3},{2,6},{3,1},{4,0},{5,7},{6,2},{7,5},{8,12},{9,11},{10,... | collective-permute-start | bytes 995336 | tf_op jit(solution)/shard_map/ppermute | solution.py:390
  102.4 49.0 %collective-permute-start.16 = (bf16[8,144,1076]{2,1,0:T(8,128)(2,1)S(1)}, bf16[8,144,1076]{2,1,0:T(8,128)(2,1)}, u32[]{:S(2)}, u32[]{:S(2)}) collective-permute-start(bf16[8,144,1076]{2,1,0:T(8,128)(2,1)S(1)} %constant_dynamic-update-slice_fusion.16.refs_2_), channel_id=1, source_target_pairs={{0,2},{1,5},{2,0},{3,7},{4,6},{5,1},{6,4},{7,3},{8,10},{9,13},{10,... | collective-permute-start | bytes 7437320 | tf_op jit(solution)/shard_map/ppermute | solution.py:390
  111.6 32.3 %collective-permute-start.14 = (bf16[8,144,288]{2,1,0:T(8,128)(2,1)S(1)}, bf16[8,144,288]{2,1,0:T(8,128)(2,1)S(1)}, u32[]{:S(2)}, u32[]{:S(2)}) collective-permute-start(bf16[8,144,288]{2,1,0:T(8,128)(2,1)S(1)} %constant_dynamic-update-slice_fusion.14.refs_0_), channel_id=1, source_target_pairs={{0,2},{1,5},{2,0},{3,7},{4,6},{5,1},{6,4},{7,3},{8,10},{9,13},{10,... | collective-permute-start | bytes 1990664 | tf_op jit(solution)/shard_map/ppermute | solution.py:390
  115.6 35.7 %collective-permute-start.15 = (bf16[4,144,1076]{2,1,0:T(8,128)(2,1)}, bf16[4,144,1076]{2,1,0:T(8,128)(2,1)}, u32[]{:S(2)}, u32[]{:S(2)}) collective-permute-start(bf16[4,144,1076]{2,1,0:T(8,128)(2,1)} %constant_dynamic-update-slice_fusion.18.refs_2_), channel_id=1, source_target_pairs={{0,8},{1,9},{2,10},{3,11},{4,12},{5,13},{6,14},{7,15},{8,0},{9,1},... | collective-permute-start | bytes 3718664 | tf_op jit(solution)/shard_map/ppermute | solution.py:390
  158.0 32.6 %collective-permute-start.19 = (bf16[4,144,1076]{2,1,0:T(8,128)(2,1)}, bf16[4,144,1076]{2,1,0:T(8,128)(2,1)}, u32[]{:S(2)}, u32[]{:S(2)}) collective-permute-start(bf16[4,144,1076]{2,1,0:T(8,128)(2,1)} %constant_dynamic-update-slice_fusion.18.refs_2_), channel_id=1, source_target_pairs={{0,2},{1,5},{2,0},{3,7},{4,6},{5,1},{6,4},{7,3},{8,10},{9,13},{10,... | collective-permute-start | bytes 3718664 | tf_op jit(solution)/shard_map/ppermute | solution.py:390
  158.5 32.1 %collective-permute-start.20 = (bf16[4,144,1076]{2,1,0:T(8,128)(2,1)}, bf16[4,144,1076]{2,1,0:T(8,128)(2,1)}, u32[]{:S(2)}, u32[]{:S(2)}) collective-permute-start(bf16[4,144,1076]{2,1,0:T(8,128)(2,1)} %collective-permute-done.15.refs_3_), channel_id=1, source_target_pairs={{0,2},{1,5},{2,0},{3,7},{4,6},{5,1},{6,4},{7,3},{8,10},{9,13},{10,... | collective-permute-start | bytes 3718664 | tf_op jit(solution)/shard_map/ppermute | solution.py:390
  190.0 34.5 %collective-permute-start.21 = (bf16[8,144,1076]{2,1,0:T(8,128)(2,1)}, bf16[8,144,1076]{2,1,0:T(8,128)(2,1)}, u32[]{:S(2)}, u32[]{:S(2)}) collective-permute-start(bf16[8,144,1076]{2,1,0:T(8,128)(2,1)} %get-tuple-element.158), channel_id=1, source_target_pairs={{0,2},{1,5},{2,0},{3,7},{4,6},{5,1},{6,4},{7,3},{8,10},{9,13},{10,... | collective-permute-start | bytes 7437320 | tf_op jit(solution)/shard_map/ppermute | solution.py:390
  228.8 35.6 %collective-permute-start.25 = (bf16[8,144,1076]{2,1,0:T(8,128)(2,1)}, bf16[8,144,1076]{2,1,0:T(8,128)(2,1)}, u32[]{:S(2)}, u32[]{:S(2)}) collective-permute-start(bf16[8,144,1076]{2,1,0:T(8,128)(2,1)} %get-tuple-element.167), channel_id=1, source_target_pairs={{0,2},{1,5},{2,0},{3,7},{4,6},{5,1},{6,4},{7,3},{8,10},{9,13},{10,... | collective-permute-start | bytes 7437320 | tf_op jit(solution)/shard_map/ppermute | solution.py:390
  229.7 34.7 %collective-permute-start.24 = (bf16[4,144,1076]{2,1,0:T(8,128)(2,1)S(1)}, bf16[4,144,1076]{2,1,0:T(8,128)(2,1)S(1)}, u32[]{:S(2)}, u32[]{:S(2)}) collective-permute-start(bf16[4,144,1076]{2,1,0:T(8,128)(2,1)S(1)} %get-tuple-element.243), channel_id=1, source_target_pairs={{0,8},{1,9},{2,10},{3,11},{4,12},{5,13},{6,14},{7,15},{8,0},{9,1},... | collective-permute-start | bytes 3718664 | tf_op jit(solution)/shard_map/ppermute | solution.py:390
  245.8 27.7 %collective-permute-start.26 = (bf16[8,144,288]{2,1,0:T(8,128)(2,1)S(1)}, bf16[8,144,288]{2,1,0:T(8,128)(2,1)}, u32[]{:S(2)}, u32[]{:S(2)}) collective-permute-start(bf16[8,144,288]{2,1,0:T(8,128)(2,1)S(1)} %get-tuple-element.175), channel_id=1, source_target_pairs={{0,2},{1,5},{2,0},{3,7},{4,6},{5,1},{6,4},{7,3},{8,10},{9,13},{10,... | collective-permute-start | bytes 1990664 | tf_op jit(solution)/shard_map/ppermute | solution.py:390
  268.8 35.6 %collective-permute-start.27 = (bf16[4,144,1076]{2,1,0:T(8,128)(2,1)}, bf16[4,144,1076]{2,1,0:T(8,128)(2,1)}, u32[]{:S(2)}, u32[]{:S(2)}) collective-permute-start(bf16[4,144,1076]{2,1,0:T(8,128)(2,1)} %get-tuple-element.241), channel_id=1, source_target_pairs={{0,4},{1,3},{2,6},{3,1},{4,0},{5,7},{6,2},{7,5},{8,12},{9,11},{10,... | collective-permute-start | bytes 3718664 | tf_op jit(solution)/shard_map/ppermute | solution.py:390
  270.6 31.6 %collective-permute-start.29 = (bf16[2,144,1076]{2,1,0:T(8,128)(2,1)S(1)}, bf16[2,144,1076]{2,1,0:T(8,128)(2,1)S(1)}, u32[]{:S(2)}, u32[]{:S(2)}) collective-permute-start(bf16[2,144,1076]{2,1,0:T(8,128)(2,1)S(1)} %get-tuple-element.249), channel_id=1, source_target_pairs={{0,16},{1,17},{2,18},{3,19},{4,20},{5,21},{6,22},{7,23},{8,24},{9,... | collective-permute-start | bytes 1859336 | tf_op jit(solution)/shard_map/ppermute | solution.py:390
  274.9 28.6 %collective-permute-start.28 = (bf16[4,144,288]{2,1,0:T(8,128)(2,1)S(1)}, bf16[4,144,288]{2,1,0:T(8,128)(2,1)S(1)}, u32[]{:S(2)}, u32[]{:S(2)}) collective-permute-start(bf16[4,144,288]{2,1,0:T(8,128)(2,1)S(1)} %get-tuple-element.253), channel_id=1, source_target_pairs={{0,4},{1,3},{2,6},{3,1},{4,0},{5,7},{6,2},{7,5},{8,12},{9,11},{10,... | collective-permute-start | bytes 995336 | tf_op jit(solution)/shard_map/ppermute | solution.py:390
  298.8 38.6 %collective-permute-start.35 = (bf16[8,144,864]{2,1,0:T(8,128)(2,1)}, bf16[8,144,864]{2,1,0:T(8,128)(2,1)S(1)}, u32[]{:S(2)}, u32[]{:S(2)}) collective-permute-start(bf16[8,144,864]{2,1,0:T(8,128)(2,1)} %get-tuple-element.189), channel_id=1, source_target_pairs={{0,2},{1,5},{2,0},{3,7},{4,6},{5,1},{6,4},{7,3},{8,10},{9,13},{10,... | collective-permute-start | bytes 5971976 | tf_op jit(solution)/shard_map/ppermute | solution.py:390
  303.7 18.2 %collective-permute-start.34 = (bf16[2,144,288]{2,1,0:T(8,128)(2,1)S(1)}, bf16[2,144,288]{2,1,0:T(8,128)(2,1)S(1)}, u32[]{:S(2)}, u32[]{:S(2)}) collective-permute-start(bf16[2,144,288]{2,1,0:T(8,128)(2,1)S(1)} %get-tuple-element.259), channel_id=1, source_target_pairs={{0,8},{1,9},{2,10},{3,11},{4,12},{5,13},{6,14},{7,15},{8,0},{9,1},... | collective-permute-start | bytes 497672 | tf_op jit(solution)/shard_map/ppermute | solution.py:390
  313.3 17.6 %collective-permute-start.33 = (bf16[2,144,1076]{2,1,0:T(8,128)(2,1)S(1)}, bf16[2,144,1076]{2,1,0:T(8,128)(2,1)S(1)}, u32[]{:S(2)}, u32[]{:S(2)}) collective-permute-start(bf16[2,144,1076]{2,1,0:T(8,128)(2,1)S(1)} %get-tuple-element.247), channel_id=1, source_target_pairs={{0,8},{1,9},{2,10},{3,11},{4,12},{5,13},{6,14},{7,15},{8,0},{9,1},... | collective-permute-start | bytes 1859336 | tf_op jit(solution)/shard_map/ppermute | solution.py:390
  313.7 20.3 %collective-permute-start.32 = (bf16[512,1152]{1,0:T(8,128)(2,1)S(1)}, bf16[512,1152]{1,0:T(8,128)(2,1)S(1)}, u32[]{:S(2)}, u32[]{:S(2)}) collective-permute-start(bf16[512,1152]{1,0:T(8,128)(2,1)S(1)} %slice.419), channel_id=1, source_target_pairs={{0,1},{1,0},{2,3},{3,2},{4,5},{5,4},{6,7},{7,6},{8,9},{9,8},{10,11... | collective-permute-start | bytes 3538952 | tf_op jit(solution)/shard_map/ppermute | solution.py:390
  321.3 12.9 %collective-permute-start.31 = (bf16[512,1152]{1,0:T(8,128)(2,1)S(1)}, bf16[512,1152]{1,0:T(8,128)(2,1)S(1)}, u32[]{:S(2)}, u32[]{:S(2)}) collective-permute-start(bf16[512,1152]{1,0:T(8,128)(2,1)S(1)} %slice.420), channel_id=1, source_target_pairs={{0,1},{1,0},{2,3},{3,2},{4,5},{5,4},{6,7},{7,6},{8,9},{9,8},{10,11... | collective-permute-start | bytes 3538952 | tf_op jit(solution)/shard_map/ppermute | solution.py:390
  321.9 21.4 %collective-permute-start.40 = (bf16[1,144,288]{2,1,0:T(8,128)(2,1)S(1)}, bf16[1,144,288]{2,1,0:T(8,128)(2,1)S(1)}, u32[]{:S(2)}, u32[]{:S(2)}) collective-permute-start(bf16[1,144,288]{2,1,0:T(8,128)(2,1)S(1)} %add_convert_fusion.26), channel_id=1, source_target_pairs={{0,16},{1,17},{2,18},{3,19},{4,20},{5,21},{6,22},{7,23},{8,24},{9,... | collective-permute-start | bytes 248840 | tf_op jit(solution)/shard_map/ppermute | solution.py:390
  331.8 16.2 %collective-permute-start.39 = (bf16[1,144,1076]{2,1,0:T(8,128)(2,1)}, bf16[1,144,1076]{2,1,0:T(8,128)(2,1)}, u32[]{:S(2)}, u32[]{:S(2)}) collective-permute-start(bf16[1,144,1076]{2,1,0:T(8,128)(2,1)} %add_convert_fusion.18), channel_id=1, source_target_pairs={{0,16},{1,17},{2,18},{3,19},{4,20},{5,21},{6,22},{7,23},{8,24},{9,... | collective-permute-start | bytes 929672 | tf_op jit(solution)/shard_map/ppermute | solution.py:390
  339.7 14.8 %collective-permute-start.38 = (bf16[4,144,864]{2,1,0:T(8,128)(2,1)}, bf16[4,144,864]{2,1,0:T(8,128)(2,1)S(1)}, u32[]{:S(2)}, u32[]{:S(2)}) collective-permute-start(bf16[4,144,864]{2,1,0:T(8,128)(2,1)} %get-tuple-element.245), channel_id=1, source_target_pairs={{0,4},{1,3},{2,6},{3,1},{4,0},{5,7},{6,2},{7,5},{8,12},{9,11},{10,... | collective-permute-start | bytes 2985992 | tf_op jit(solution)/shard_map/ppermute | solution.py:390
  354.8 12.6 %collective-permute-start.42 = (bf16[2,144,864]{2,1,0:T(8,128)(2,1)S(1)}, bf16[2,144,864]{2,1,0:T(8,128)(2,1)S(1)}, u32[]{:S(2)}, u32[]{:S(2)}) collective-permute-start(bf16[2,144,864]{2,1,0:T(8,128)(2,1)S(1)} %get-tuple-element.251), channel_id=1, source_target_pairs={{0,8},{1,9},{2,10},{3,11},{4,12},{5,13},{6,14},{7,15},{8,0},{9,1},... | collective-permute-start | bytes 1493000 | tf_op jit(solution)/shard_map/ppermute | solution.py:390
  (101 other events, 1111.5 us)

commit v2 on v1

--- a/solution.py
+++ b/solution.py
@@ -516,7 +516,7 @@
     last, near = plan.stages, max(plan.stages - 1, 0)
     far = max(plan.stages - 2, 0)
     first = max(plan.stages - 3, 0)
-    gather_qkv = Gather(plan, order, jnp.concatenate([low(w_query), low(w_key), low(w_value)], axis=1))
+    gather_qkv = Gather(plan, order, low(jnp.concatenate([w_query, w_key, w_value], axis=1)))
     gather_out = Gather(plan, order, low(w_out).T)
     gather_up = Gather(plan, order, low(w_up))
     gather_down = Gather(plan, order, low(w_down).T, "near", joined=False)

time: 385 us -> 384 us (level)
  no operation moved by 1% of the time
where the time goes in v2:
time: 384 us; the launch traced here: 380 us
  Pallas kernels  128 us (33%)
  waiting for transfers between devices  118 us (31%)
  starting transfers between devices  54.4 us (14%)
  other arithmetic  34.3 us (9%)
  matrix products  23.7 us (6%)
  local copies, waits for them, and re-layouts  20 us (5%)
    ppermute x46, waiting for transfers between devices, permute(): return lax.ppermute(values, ('dp', 'tensor'), pairs)  118 us
    ppermute x46, starting transfers between devices, permute(): return lax.ppermute(values, ('dp', 'tensor'), pairs)  54.4 us
    pallas_call x4, Pallas kernels, weight_grad(): pl.pallas_call(functools.partial(weight_grad_body, images, n_dp, half), i...  36.6 us
    pallas_call x2, Pallas kernels, attend_backward(): pl.pallas_call(functools.partial(attend_backward_body, heads), in_specs=[...  29.3 us
    dot_general x8, matrix products, dot(): return lax.dot_general(left, right, dims, preferred_element_type=F32)  23.7 us
    pallas_call x2, Pallas kernels, attend_forward(): kernel_call(functools.partial(attend_forward_body, heads, len(parts)), 'a...  23 us
    pallas_call x2, Pallas kernels, up(): kernel_call(functools.partial(up_body, len(parts)), 'up', 1, len(parts),...  19.1 us
    pallas_call x2, Pallas kernels, pre_grad(): kernel_call(functools.partial(pre_grad_body, len(parts)), 'pre_grad', 0,...  15.3 us
  transfers between devices with their start and end apart: 46, of which 26 were waited for; matrix products, arithmetic and copies ran while one was open for 15% of the time, Pallas kernels for 34%

profile of v2, /device:TPU:0, one launch (start us, length us, event | category | flops | bytes accessed | tf_op | source)
XLA Modules:
  0.0 380.1 jit_solution(16065560092642674497)
XLA Ops:
  3.0 4.1 %collective-permute-start = (bf16[1,144,864]{2,1,0:T(8,128)(2,1)S(1)}, bf16[1,144,864]{2,1,0:T(8,128)(2,1)S(1)}, u32[]{:S(2)}, u32[]{:S(2)}) collective-permute-start(bf16[1,144,864]{2,1,0:T(8,128)(2,1)S(1)} %pad_maximum_fusion.1), channel_id=1, source_target_pairs={{0,16},{1,17},{2,18},{3,19},{4,20},{5,21},{6,22},{7,23},{8,24},{9,... | collective-permute-start | bytes 746504 | tf_op jit(solution)/shard_map/ppermute | solution.py:390
  9.5 9.3 %collective-permute-done = bf16[1,144,864]{2,1,0:T(8,128)(2,1)S(1)} collective-permute-done((bf16[1,144,864]{2,1,0:T(8,128)(2,1)S(1)}, bf16[1,144,864]{2,1,0:T(8,128)(2,1)S(1)}, u32[]{:S(2)}, u32[]{:S(2)}) %collective-permute-start) | collective-permute-done | bytes 248864 | tf_op jit(solution)/shard_map/ppermute | solution.py:390
  21.4 3.4 collective-permute-start.3
  27.0 6.3 %collective-permute-done.3 = bf16[1,144,288]{2,1,0:T(8,128)(2,1)S(1)} collective-permute-done((bf16[1,144,288]{2,1,0:T(8,128)(2,1)S(1)}, bf16[1,144,288]{2,1,0:T(8,128)(2,1)S(1)}, u32[]{:S(2)}, u32[]{:S(2)}) %collective-permute-start.3) | collective-permute-done | bytes 82976 | tf_op jit(solution)/shard_map/ppermute | solution.py:390
  42.8 8.3 %collective-permute-done.9 = bf16[2,144,288]{2,1,0:T(8,128)(2,1)S(1)} collective-permute-done((bf16[2,144,288]{2,1,0:T(8,128)(2,1)S(1)}, bf16[2,144,288]{2,1,0:T(8,128)(2,1)S(1)}, u32[]{:S(2)}, u32[]{:S(2)}) %collective-permute-start.9) | collective-permute-done | bytes 165920 | tf_op jit(solution)/shard_map/ppermute | solution.py:390
  51.1 3.1 collective-permute-done.2
  61.3 15.1 %collective-permute-done.8 = bf16[2,144,1076]{2,1,0:T(8,128)(2,1)S(1)} collective-permute-done((bf16[2,144,1076]{2,1,0:T(8,128)(2,1)S(1)}, bf16[2,144,1076]{2,1,0:T(8,128)(2,1)S(1)}, u32[]{:S(2)}, u32[]{:S(2)}) %collective-permute-start.8) | collective-permute-done | bytes 619808 | tf_op jit(solution)/shard_map/ppermute | solution.py:390
  76.5 6.6 %collective-permute-done.10.refs_3_ = bf16[8,144,864]{2,1,0:T(8,128)(2,1)} collective-permute-done((bf16[8,144,864]{2,1,0:T(8,128)(2,1)}, bf16[8,144,864]{2,1,0:T(8,128)(2,1)}, u32[]{:S(2)}, u32[]{:S(2)}) %collective-permute-start.10) | collective-permute-done | bytes 1990688 | tf_op jit(solution)/shard_map/ppermute | solution.py:390
  87.7 11.5 %attend_forward.2 = (bf16[1024,864]{1,0:T(8,128)(2,1)}, bf16[1024,288]{1,0:T(8,128)(2,1)S(1)}, f32[4,1024]{1,0:T(4,128)S(1)}, bf16[1152,864]{1,0:T(8,128)(2,1)}) custom-call(s32[8]{0:T(128)S(1)} %get-tuple-element.148.table_ref, f32[1,864]{1,0:T(1,128)S(1)} %broadcast_in_dim.274.bias_ref, bf16[512,1152]{1,0:T(8,128)(2,1)S(1)} %fusion.7.refs_0_, ...), custom_call_target="tpu_custom_call" | custom-call | flops 8480882688 | bytes 6356992 | tf_op jit(solution)/shard_map/attend_forward/pallas_call | solution.py:161
  102.4 8.4 %collective-permute-done.11 = bf16[4,144,288]{2,1,0:T(8,128)(2,1)S(1)} collective-permute-done((bf16[4,144,288]{2,1,0:T(8,128)(2,1)S(1)}, bf16[4,144,288]{2,1,0:T(8,128)(2,1)S(1)}, u32[]{:S(2)}, u32[]{:S(2)}) %collective-permute-start.11) | collective-permute-done | bytes 331808 | tf_op jit(solution)/shard_map/ppermute | solution.py:390
  115.6 11.5 %attend_forward.3 = (bf16[1024,864]{1,0:T(8,128)(2,1)}, bf16[1024,288]{1,0:T(8,128)(2,1)S(1)}, f32[4,1024]{1,0:T(4,128)S(1)}, bf16[1152,864]{1,0:T(8,128)(2,1)}) custom-call(s32[8]{0:T(128)S(1)} %get-tuple-element.150.table_ref, f32[1,864]{1,0:T(1,128)S(1)} %broadcast_in_dim.278.bias_ref, bf16[512,1152]{1,0:T(8,128)(2,1)S(1)} %fusion.7.refs_0_, ...), custom_call_target="tpu_custom_call" | custom-call | flops 8480882688 | bytes 6356992 | tf_op jit(solution)/shard_map/attend_forward/pallas_call | solution.py:161
  127.2 16.0 %collective-permute-done.14.refs_1_ = bf16[8,144,288]{2,1,0:T(8,128)(2,1)S(1)} collective-permute-done((bf16[8,144,288]{2,1,0:T(8,128)(2,1)S(1)}, bf16[8,144,288]{2,1,0:T(8,128)(2,1)S(1)}, u32[]{:S(2)}, u32[]{:S(2)}) %collective-permute-start.14) | collective-permute-done | bytes 663584 | tf_op jit(solution)/shard_map/ppermute | solution.py:390
  160.1 9.3 %up.2 = (bf16[1024,1076]{1,0:T(8,128)(2,1)}, bf16[1024,1076]{1,0:T(8,128)(2,1)}, bf16[1152,1076]{1,0:T(8,128)(2,1)}) custom-call(s32[8]{0:T(128)S(1)} %copy-done.21, f32[1,1076]{1,0:T(1,128)S(1)} %broadcast_in_dim.279.bias_ref, bf16[512,1152]{1,0:T(8,128)(2,1)} %add_convert_fusion.6.refs_0_, bf16[512,1152]{1,0:T(8,128)(2,1)} %collective-permute-done.18.refs_1_, ...), custom_call_target="tpu_custom_call" | custom-call | flops 2538602496 | bytes 9365504 | tf_op jit(solution)/shard_map/up/pallas_call | solution.py:221
  169.4 9.8 %up.3 = (bf16[1024,1076]{1,0:T(8,128)(2,1)}, bf16[1024,1076]{1,0:T(8,128)(2,1)}, bf16[1152,1076]{1,0:T(8,128)(2,1)}) custom-call(s32[8]{0:T(128)S(1)} %copy-done.19, f32[1,1076]{1,0:T(1,128)S(1)} %broadcast_in_dim.280.bias_ref, bf16[512,1152]{1,0:T(8,128)(2,1)} %add_convert_fusion.6.refs_0_, bf16[512,1152]{1,0:T(8,128)(2,1)} %collective-permute-done.18.refs_1_, ...), custom_call_target="tpu_custom_call" | custom-call | flops 2538602496 | bytes 9365504 | tf_op jit(solution)/shard_map/up/pallas_call | solution.py:221
  179.2 10.0 %grad_down.1 = (bf16[8,144,1076]{2,1,0:T(8,128)(2,1)}, bf16[8,144,1076]{2,1,0:T(8,128)(2,1)}) custom-call(s32[16]{0:T(128)S(1)} %select_n.272.table_ref, bf16[512,1152]{1,0:T(8,128)(2,1)S(1)} %copy-done, bf16[512,1152]{1,0:T(8,128)(2,1)S(1)} %collective-permute-done.6.refs_1_, bf16[1024,1076]{1,0:T(8,128)(2,1)} %get-tuple-element.202.refs_2_, ...), custom_call_target="tpu_custom_call" | custom-call | tf_op jit(solution)/shard_map/grad_down/pallas_call | solution.py:354
  189.9 7.6 %pre_grad.2 = (bf16[1024,1076]{1,0:T(8,128)(2,1)}, f32[1,1076]{1,0:T(1,128)S(1)}, bf16[1152,1076]{1,0:T(8,128)(2,1)}) custom-call(s32[8]{0:T(128)S(1)} %get-tuple-element.159.table_ref, bf16[1024,1076]{1,0:T(8,128)(2,1)} %get-tuple-element.160.slope_in, bf16[512,1152]{1,0:T(8,128)(2,1)S(1)} %copy-done, bf16[512,1152]{1,0:T(8,128)(2,1)S(1)} %collective-permute-done.6.refs_1_, ...), custom_call_target="tpu_custom_call" | custom-call | flops 2538602496 | bytes 7166160 | tf_op jit(solution)/shard_map/pre_grad/pallas_call | solution.py:252
  197.5 7.7 %pre_grad.3 = (bf16[1024,1076]{1,0:T(8,128)(2,1)}, f32[1,1076]{1,0:T(1,128)S(1)}, bf16[1152,1076]{1,0:T(8,128)(2,1)}) custom-call(s32[8]{0:T(128)S(1)} %get-tuple-element.164.table_ref, bf16[1024,1076]{1,0:T(8,128)(2,1)} %get-tuple-element.165.slope_in, bf16[512,1152]{1,0:T(8,128)(2,1)S(1)} %copy-done, bf16[512,1152]{1,0:T(8,128)(2,1)S(1)} %collective-permute-done.6.refs_1_, ...), custom_call_target="tpu_custom_call" | custom-call | flops 2538602496 | bytes 7166160 | tf_op jit(solution)/shard_map/pre_grad/pallas_call | solution.py:252
  205.2 10.8 %grad_up.1 = (bf16[8,144,1076]{2,1,0:T(8,128)(2,1)}, bf16[8,144,1076]{2,1,0:T(8,128)(2,1)}) custom-call(s32[16]{0:T(128)S(1)} %select_n.266.table_ref, bf16[512,1152]{1,0:T(8,128)(2,1)} %add_convert_fusion.6.refs_0_, bf16[512,1152]{1,0:T(8,128)(2,1)} %collective-permute-done.18.refs_1_, bf16[1024,1076]{1,0:T(8,128)(2,1)} %get-tuple-element.162.refs_2_, ...), custom_call_target="tpu_custom_call" | custom-call | tf_op jit(solution)/shard_map/grad_up/pallas_call | solution.py:354
  216.1 3.5 fusion.35
  219.6 4.1 %convolution_add_fusion.3 = f32[1024,1152]{1,0:T(8,128)S(1)} fusion(f32[1024,1152]{1,0:T(8,128)S(1)} %fusion.35, bf16[1024,1076]{1,0:T(8,128)(2,1)S(1)} %copy-done.40, bf16[1152,1076]{1,0:T(8,128)(2,1)S(1)} %copy-done.83), kind=kOutput, calls=%fused_computation.3 | convolution fusion | flops 2539782144 | bytes 14119936 | tf_op jit(solution)/shard_map/dot_general | solution.py:29
  223.7 3.4 add_convert_fusion.2
  237.7 7.4 %grad_out.1 = (bf16[8,144,288]{2,1,0:T(8,128)(2,1)S(1)}, bf16[8,144,288]{2,1,0:T(8,128)(2,1)S(1)}) custom-call(s32[16]{0:T(128)S(1)} %select_n.266.table_ref, bf16[512,1152]{1,0:T(8,128)(2,1)} %copy-done.1, bf16[512,1152]{1,0:T(8,128)(2,1)} %copy-done.3, bf16[1024,288]{1,0:T(8,128)(2,1)S(1)} %copy-done.10, bf16[1024,288]{1,0:T(8,128)(2,1)S(1)} %copy-done.8), custom_call_target="tpu_custom_call" | custom-call | tf_op jit(solution)/shard_map/grad_out/pallas_call | solution.py:354
  248.9 14.8 %attend_backward.2.refs_2_ = bf16[1024,864]{1,0:T(8,128)(2,1)} custom-call(f32[4,1024]{1,0:T(4,128)S(1)} %copy-done.17, bf16[1024,864]{1,0:T(8,128)(2,1)} %get-tuple-element.177.qkv_in, bf16[1024,288]{1,0:T(8,128)(2,1)S(1)} %copy-done.10, bf16[1152,288]{1,0:T(8,128)(2,1)S(1)} %copy-done.6, bf16[512,1152]{1,0:T(8,128)(2,1)S(1)} %copy-done.2, ...), custom_call_target="tpu_custom_call" | custom-call | tf_op jit(solution)/shard_map/attend_backward/pallas_call | solution.py:291
  263.7 4.4 %add_convert_fusion = (bf16[4,144,1076]{2,1,0:T(8,128)(2,1)}, bf16[4,144,1076]{2,1,0:T(8,128)(2,1)}) fusion(bf16[8,144,1076]{2,1,0:T(8,128)(2,1)} %collective-permute-done.25, bf16[8,144,1076]{2,1,0:T(8,128)(2,1)S(1)} %copy-done.36), kind=kLoop, calls=%fused_computation.19 | loop fusion | flops 4958208 | bytes 7437312 | tf_op jit(solution)/shard_map/convert_element_type | solution.py:465
  275.1 14.5 %attend_backward.3.refs_3_ = bf16[1024,864]{1,0:T(8,128)(2,1)} custom-call(f32[4,1024]{1,0:T(4,128)S(1)} %get-tuple-element.186.lse_ref, bf16[1024,864]{1,0:T(8,128)(2,1)} %get-tuple-element.187.qkv_in, bf16[1024,288]{1,0:T(8,128)(2,1)S(1)} %copy-done.8, bf16[1152,288]{1,0:T(8,128)(2,1)S(1)} %place_out.3.out_in, bf16[512,1152]{1,0:T(8,128)(2,1)S(1)} %copy-done.2, ...), custom_call_target="tpu_custom_call" | custom-call | tf_op jit(solution)/shard_map/attend_backward/pallas_call | solution.py:291
  289.6 8.4 %grad_qkv.1 = (bf16[8,144,864]{2,1,0:T(8,128)(2,1)}, bf16[8,144,864]{2,1,0:T(8,128)(2,1)}) custom-call(s32[16]{0:T(128)S(1)} %select_n.266.table_ref, bf16[512,1152]{1,0:T(8,128)(2,1)S(1)} %copy-done.12, bf16[512,1152]{1,0:T(8,128)(2,1)S(1)} %copy-done.15, bf16[1024,864]{1,0:T(8,128)(2,1)} %attend_backward.2.refs_2_, bf16[1024,864]{1,0:T(8,128)(2,1)} %attend_backward.3.refs_3_), custom_call_target="tpu_custom_call" | custom-call | tf_op jit(solution)/shard_map/grad_qkv/pallas_call | solution.py:354
  313.0 3.6 fusion.37
  316.6 3.9 %convolution_add_fusion.2 = f32[1024,1152]{1,0:T(8,128)S(1)} fusion(f32[1024,1152]{1,0:T(8,128)S(1)} %fusion.37, bf16[1024,1076]{1,0:T(8,128)(2,1)S(1)} %copy-done.38, bf16[1152,1076]{1,0:T(8,128)(2,1)S(1)} %copy-done.81), kind=kOutput, calls=%fused_computation.2 | convolution fusion | flops 2539782144 | bytes 14119936 | tf_op jit(solution)/shard_map/dot_general | solution.py:29
  321.2 3.4 collective-permute-start.40
  324.7 5.5 %collective-permute-done.33 = bf16[2,144,1076]{2,1,0:T(8,128)(2,1)S(1)} collective-permute-done((bf16[2,144,1076]{2,1,0:T(8,128)(2,1)S(1)}, bf16[2,144,1076]{2,1,0:T(8,128)(2,1)S(1)}, u32[]{:S(2)}, u32[]{:S(2)}) %collective-permute-start.33) | collective-permute-done | bytes 619808 | tf_op jit(solution)/shard_map/ppermute | solution.py:390
  349.6 4.2 %collective-permute-done.38 = bf16[4,144,864]{2,1,0:T(8,128)(2,1)S(1)} collective-permute-done((bf16[4,144,864]{2,1,0:T(8,128)(2,1)}, bf16[4,144,864]{2,1,0:T(8,128)(2,1)S(1)}, u32[]{:S(2)}, u32[]{:S(2)}) %collective-permute-start.38) | collective-permute-done | bytes 995360 | tf_op jit(solution)/shard_map/ppermute | solution.py:390
  356.6 10.2 %collective-permute-done.41 = f32[14336]{0:T(1024)S(1)} collective-permute-done((f32[14336]{0:T(1024)S(1)}, f32[14336]{0:T(1024)S(1)}, u32[]{:S(2)}, u32[]{:S(2)}) %collective-permute-start.41) | collective-permute-done | bytes 57376 | tf_op jit(solution)/shard_map/ppermute | solution.py:390
  (365 shorter events, 127.7 us)
Async XLA Ops:
  3.0 15.8 %collective-permute-start = (bf16[1,144,864]{2,1,0:T(8,128)(2,1)S(1)}, bf16[1,144,864]{2,1,0:T(8,128)(2,1)S(1)}, u32[]{:S(2)}, u32[]{:S(2)}) collective-permute-start(bf16[1,144,864]{2,1,0:T(8,128)(2,1)S(1)} %pad_maximum_fusion.1), channel_id=1, source_target_pairs={{0,16},{1,17},{2,18},{3,19},{4,20},{5,21},{6,22},{7,23},{8,24},{9,... | collective-permute-start | bytes 746504 | tf_op jit(solution)/shard_map/ppermute | solution.py:390
  8.9 25.4 %collective-permute-start.5 = (bf16[512,1152]{1,0:T(8,128)(2,1)S(1)}, bf16[512,1152]{1,0:T(8,128)(2,1)S(1)}, u32[]{:S(2)}, u32[]{:S(2)}) collective-permute-start(bf16[512,1152]{1,0:T(8,128)(2,1)S(1)} %fusion.7.refs_0_), channel_id=1, source_target_pairs={{0,1},{1,0},{2,3},{3,2},{4,5},{5,4},{6,7},{7,6},{8,9},{9,8},{10,11... | collective-permute-start | bytes 3538952 | tf_op jit(solution)/shard_map/ppermute | solution.py:390
  9.0 26.3 %collective-permute-start.6 = (bf16[512,1152]{1,0:T(8,128)(2,1)S(1)}, bf16[512,1152]{1,0:T(8,128)(2,1)S(1)}, u32[]{:S(2)}, u32[]{:S(2)}) collective-permute-start(bf16[512,1152]{1,0:T(8,128)(2,1)S(1)} %copy-done), channel_id=1, source_target_pairs={{0,1},{1,0},{2,3},{3,2},{4,5},{5,4},{6,7},{7,6},{8,9},{9,8},{10,11... | collective-permute-start | bytes 3538952 | tf_op jit(solution)/shard_map/ppermute | solution.py:390
  19.0 15.4 %collective-permute-start.1 = (bf16[2,144,864]{2,1,0:T(8,128)(2,1)S(1)}, bf16[2,144,864]{2,1,0:T(8,128)(2,1)S(1)}, u32[]{:S(2)}, u32[]{:S(2)}) collective-permute-start(bf16[2,144,864]{2,1,0:T(8,128)(2,1)S(1)} %pad_maximum_fusion), channel_id=1, source_target_pairs={{0,8},{1,9},{2,10},{3,11},{4,12},{5,13},{6,14},{7,15},{8,0},{9,1},... | collective-permute-start | bytes 1493000 | tf_op jit(solution)/shard_map/ppermute | solution.py:390
  35.5 19.4 %collective-permute-start.7 = (bf16[4,144,864]{2,1,0:T(8,128)(2,1)S(1)}, bf16[4,144,864]{2,1,0:T(8,128)(2,1)S(1)}, u32[]{:S(2)}, u32[]{:S(2)}) collective-permute-start(bf16[4,144,864]{2,1,0:T(8,128)(2,1)S(1)} %constant_dynamic-update-slice_fusion), channel_id=1, source_target_pairs={{0,4},{1,3},{2,6},{3,1},{4,0},{5,7},{6,2},{7,5},{8,12},{9,11},{10,... | collective-permute-start | bytes 2985992 | tf_op jit(solution)/shard_map/ppermute | solution.py:390
  37.6 16.6 %collective-permute-start.2 = (bf16[1,144,1076]{2,1,0:T(8,128)(2,1)S(1)}, bf16[1,144,1076]{2,1,0:T(8,128)(2,1)S(1)}, u32[]{:S(2)}, u32[]{:S(2)}) collective-permute-start(bf16[1,144,1076]{2,1,0:T(8,128)(2,1)S(1)} %convert_bitcast_fusion.1), channel_id=1, source_target_pairs={{0,16},{1,17},{2,18},{3,19},{4,20},{5,21},{6,22},{7,23},{8,24},{9,... | collective-permute-start | bytes 929672 | tf_op jit(solution)/shard_map/ppermute | solution.py:390
  57.1 26.0 %collective-permute-start.10 = (bf16[8,144,864]{2,1,0:T(8,128)(2,1)}, bf16[8,144,864]{2,1,0:T(8,128)(2,1)}, u32[]{:S(2)}, u32[]{:S(2)}) collective-permute-start(bf16[8,144,864]{2,1,0:T(8,128)(2,1)} %constant_dynamic-update-slice_fusion.6.refs_2_), channel_id=1, source_target_pairs={{0,2},{1,5},{2,0},{3,7},{4,6},{5,1},{6,4},{7,3},{8,10},{9,13},{10,... | collective-permute-start | bytes 5971976 | tf_op jit(solution)/shard_map/ppermute | solution.py:390
  59.9 16.6 %collective-permute-start.8 = (bf16[2,144,1076]{2,1,0:T(8,128)(2,1)S(1)}, bf16[2,144,1076]{2,1,0:T(8,128)(2,1)S(1)}, u32[]{:S(2)}, u32[]{:S(2)}) collective-permute-start(bf16[2,144,1076]{2,1,0:T(8,128)(2,1)S(1)} %constant_dynamic-update-slice_fusion.2), channel_id=1, source_target_pairs={{0,8},{1,9},{2,10},{3,11},{4,12},{5,13},{6,14},{7,15},{8,0},{9,1},... | collective-permute-start | bytes 1859336 | tf_op jit(solution)/shard_map/ppermute | solution.py:390
  83.2 18.1 %collective-permute-start.12 = (bf16[4,144,1076]{2,1,0:T(8,128)(2,1)S(1)}, bf16[4,144,1076]{2,1,0:T(8,128)(2,1)S(1)}, u32[]{:S(2)}, u32[]{:S(2)}) collective-permute-start(bf16[4,144,1076]{2,1,0:T(8,128)(2,1)S(1)} %constant_dynamic-update-slice_fusion.8), channel_id=1, source_target_pairs={{0,4},{1,3},{2,6},{3,1},{4,0},{5,7},{6,2},{7,5},{8,12},{9,11},{10,... | collective-permute-start | bytes 3718664 | tf_op jit(solution)/shard_map/ppermute | solution.py:390
  84.8 28.2 %collective-permute-start.13 = (bf16[2,144,1076]{2,1,0:T(8,128)(2,1)S(1)}, bf16[2,144,1076]{2,1,0:T(8,128)(2,1)S(1)}, u32[]{:S(2)}, u32[]{:S(2)}) collective-permute-start(bf16[2,144,1076]{2,1,0:T(8,128)(2,1)S(1)} %constant_dynamic-update-slice_fusion.10), channel_id=1, source_target_pairs={{0,16},{1,17},{2,18},{3,19},{4,20},{5,21},{6,22},{7,23},{8,24},{9,... | collective-permute-start | bytes 1859336 | tf_op jit(solution)/shard_map/ppermute | solution.py:390
  87.1 23.7 %collective-permute-start.11 = (bf16[4,144,288]{2,1,0:T(8,128)(2,1)S(1)}, bf16[4,144,288]{2,1,0:T(8,128)(2,1)S(1)}, u32[]{:S(2)}, u32[]{:S(2)}) collective-permute-start(bf16[4,144,288]{2,1,0:T(8,128)(2,1)S(1)} %constant_dynamic-update-slice_fusion.12), channel_id=1, source_target_pairs={{0,4},{1,3},{2,6},{3,1},{4,0},{5,7},{6,2},{7,5},{8,12},{9,11},{10,... | collective-permute-start | bytes 995336 | tf_op jit(solution)/shard_map/ppermute | solution.py:390
  101.6 49.0 %collective-permute-start.16 = (bf16[8,144,1076]{2,1,0:T(8,128)(2,1)S(1)}, bf16[8,144,1076]{2,1,0:T(8,128)(2,1)}, u32[]{:S(2)}, u32[]{:S(2)}) collective-permute-start(bf16[8,144,1076]{2,1,0:T(8,128)(2,1)S(1)} %constant_dynamic-update-slice_fusion.16.refs_2_), channel_id=1, source_target_pairs={{0,2},{1,5},{2,0},{3,7},{4,6},{5,1},{6,4},{7,3},{8,10},{9,13},{10,... | collective-permute-start | bytes 7437320 | tf_op jit(solution)/shard_map/ppermute | solution.py:390
  110.9 32.3 %collective-permute-start.14 = (bf16[8,144,288]{2,1,0:T(8,128)(2,1)S(1)}, bf16[8,144,288]{2,1,0:T(8,128)(2,1)S(1)}, u32[]{:S(2)}, u32[]{:S(2)}) collective-permute-start(bf16[8,144,288]{2,1,0:T(8,128)(2,1)S(1)} %constant_dynamic-update-slice_fusion.14.refs_0_), channel_id=1, source_target_pairs={{0,2},{1,5},{2,0},{3,7},{4,6},{5,1},{6,4},{7,3},{8,10},{9,13},{10,... | collective-permute-start | bytes 1990664 | tf_op jit(solution)/shard_map/ppermute | solution.py:390
  114.9 35.7 %collective-permute-start.15 = (bf16[4,144,1076]{2,1,0:T(8,128)(2,1)}, bf16[4,144,1076]{2,1,0:T(8,128)(2,1)}, u32[]{:S(2)}, u32[]{:S(2)}) collective-permute-start(bf16[4,144,1076]{2,1,0:T(8,128)(2,1)} %constant_dynamic-update-slice_fusion.18.refs_2_), channel_id=1, source_target_pairs={{0,8},{1,9},{2,10},{3,11},{4,12},{5,13},{6,14},{7,15},{8,0},{9,1},... | collective-permute-start | bytes 3718664 | tf_op jit(solution)/shard_map/ppermute | solution.py:390
  157.2 32.6 %collective-permute-start.19 = (bf16[4,144,1076]{2,1,0:T(8,128)(2,1)}, bf16[4,144,1076]{2,1,0:T(8,128)(2,1)}, u32[]{:S(2)}, u32[]{:S(2)}) collective-permute-start(bf16[4,144,1076]{2,1,0:T(8,128)(2,1)} %constant_dynamic-update-slice_fusion.18.refs_2_), channel_id=1, source_target_pairs={{0,2},{1,5},{2,0},{3,7},{4,6},{5,1},{6,4},{7,3},{8,10},{9,13},{10,... | collective-permute-start | bytes 3718664 | tf_op jit(solution)/shard_map/ppermute | solution.py:390
  157.7 32.1 %collective-permute-start.20 = (bf16[4,144,1076]{2,1,0:T(8,128)(2,1)}, bf16[4,144,1076]{2,1,0:T(8,128)(2,1)}, u32[]{:S(2)}, u32[]{:S(2)}) collective-permute-start(bf16[4,144,1076]{2,1,0:T(8,128)(2,1)} %collective-permute-done.15.refs_3_), channel_id=1, source_target_pairs={{0,2},{1,5},{2,0},{3,7},{4,6},{5,1},{6,4},{7,3},{8,10},{9,13},{10,... | collective-permute-start | bytes 3718664 | tf_op jit(solution)/shard_map/ppermute | solution.py:390
  189.2 34.5 %collective-permute-start.21 = (bf16[8,144,1076]{2,1,0:T(8,128)(2,1)}, bf16[8,144,1076]{2,1,0:T(8,128)(2,1)}, u32[]{:S(2)}, u32[]{:S(2)}) collective-permute-start(bf16[8,144,1076]{2,1,0:T(8,128)(2,1)} %get-tuple-element.158), channel_id=1, source_target_pairs={{0,2},{1,5},{2,0},{3,7},{4,6},{5,1},{6,4},{7,3},{8,10},{9,13},{10,... | collective-permute-start | bytes 7437320 | tf_op jit(solution)/shard_map/ppermute | solution.py:390
  228.1 35.6 %collective-permute-start.25 = (bf16[8,144,1076]{2,1,0:T(8,128)(2,1)}, bf16[8,144,1076]{2,1,0:T(8,128)(2,1)}, u32[]{:S(2)}, u32[]{:S(2)}) collective-permute-start(bf16[8,144,1076]{2,1,0:T(8,128)(2,1)} %get-tuple-element.167), channel_id=1, source_target_pairs={{0,2},{1,5},{2,0},{3,7},{4,6},{5,1},{6,4},{7,3},{8,10},{9,13},{10,... | collective-permute-start | bytes 7437320 | tf_op jit(solution)/shard_map/ppermute | solution.py:390
  228.9 34.7 %collective-permute-start.24 = (bf16[4,144,1076]{2,1,0:T(8,128)(2,1)S(1)}, bf16[4,144,1076]{2,1,0:T(8,128)(2,1)S(1)}, u32[]{:S(2)}, u32[]{:S(2)}) collective-permute-start(bf16[4,144,1076]{2,1,0:T(8,128)(2,1)S(1)} %get-tuple-element.243), channel_id=1, source_target_pairs={{0,8},{1,9},{2,10},{3,11},{4,12},{5,13},{6,14},{7,15},{8,0},{9,1},... | collective-permute-start | bytes 3718664 | tf_op jit(solution)/shard_map/ppermute | solution.py:390
  245.1 27.7 %collective-permute-start.26 = (bf16[8,144,288]{2,1,0:T(8,128)(2,1)S(1)}, bf16[8,144,288]{2,1,0:T(8,128)(2,1)}, u32[]{:S(2)}, u32[]{:S(2)}) collective-permute-start(bf16[8,144,288]{2,1,0:T(8,128)(2,1)S(1)} %get-tuple-element.175), channel_id=1, source_target_pairs={{0,2},{1,5},{2,0},{3,7},{4,6},{5,1},{6,4},{7,3},{8,10},{9,13},{10,... | collective-permute-start | bytes 1990664 | tf_op jit(solution)/shard_map/ppermute | solution.py:390
  268.1 35.6 %collective-permute-start.27 = (bf16[4,144,1076]{2,1,0:T(8,128)(2,1)}, bf16[4,144,1076]{2,1,0:T(8,128)(2,1)}, u32[]{:S(2)}, u32[]{:S(2)}) collective-permute-start(bf16[4,144,1076]{2,1,0:T(8,128)(2,1)} %get-tuple-element.241), channel_id=1, source_target_pairs={{0,4},{1,3},{2,6},{3,1},{4,0},{5,7},{6,2},{7,5},{8,12},{9,11},{10,... | collective-permute-start | bytes 3718664 | tf_op jit(solution)/shard_map/ppermute | solution.py:390
  269.9 31.6 %collective-permute-start.29 = (bf16[2,144,1076]{2,1,0:T(8,128)(2,1)S(1)}, bf16[2,144,1076]{2,1,0:T(8,128)(2,1)S(1)}, u32[]{:S(2)}, u32[]{:S(2)}) collective-permute-start(bf16[2,144,1076]{2,1,0:T(8,128)(2,1)S(1)} %get-tuple-element.249), channel_id=1, source_target_pairs={{0,16},{1,17},{2,18},{3,19},{4,20},{5,21},{6,22},{7,23},{8,24},{9,... | collective-permute-start | bytes 1859336 | tf_op jit(solution)/shard_map/ppermute | solution.py:390
  274.2 28.6 %collective-permute-start.28 = (bf16[4,144,288]{2,1,0:T(8,128)(2,1)S(1)}, bf16[4,144,288]{2,1,0:T(8,128)(2,1)S(1)}, u32[]{:S(2)}, u32[]{:S(2)}) collective-permute-start(bf16[4,144,288]{2,1,0:T(8,128)(2,1)S(1)} %get-tuple-element.253), channel_id=1, source_target_pairs={{0,4},{1,3},{2,6},{3,1},{4,0},{5,7},{6,2},{7,5},{8,12},{9,11},{10,... | collective-permute-start | bytes 995336 | tf_op jit(solution)/shard_map/ppermute | solution.py:390
  298.1 38.6 %collective-permute-start.35 = (bf16[8,144,864]{2,1,0:T(8,128)(2,1)}, bf16[8,144,864]{2,1,0:T(8,128)(2,1)S(1)}, u32[]{:S(2)}, u32[]{:S(2)}) collective-permute-start(bf16[8,144,864]{2,1,0:T(8,128)(2,1)} %get-tuple-element.189), channel_id=1, source_target_pairs={{0,2},{1,5},{2,0},{3,7},{4,6},{5,1},{6,4},{7,3},{8,10},{9,13},{10,... | collective-permute-start | bytes 5971976 | tf_op jit(solution)/shard_map/ppermute | solution.py:390
  303.0 18.2 %collective-permute-start.34 = (bf16[2,144,288]{2,1,0:T(8,128)(2,1)S(1)}, bf16[2,144,288]{2,1,0:T(8,128)(2,1)S(1)}, u32[]{:S(2)}, u32[]{:S(2)}) collective-permute-start(bf16[2,144,288]{2,1,0:T(8,128)(2,1)S(1)} %get-tuple-element.259), channel_id=1, source_target_pairs={{0,8},{1,9},{2,10},{3,11},{4,12},{5,13},{6,14},{7,15},{8,0},{9,1},... | collective-permute-start | bytes 497672 | tf_op jit(solution)/shard_map/ppermute | solution.py:390
  312.6 17.6 %collective-permute-start.33 = (bf16[2,144,1076]{2,1,0:T(8,128)(2,1)S(1)}, bf16[2,144,1076]{2,1,0:T(8,128)(2,1)S(1)}, u32[]{:S(2)}, u32[]{:S(2)}) collective-permute-start(bf16[2,144,1076]{2,1,0:T(8,128)(2,1)S(1)} %get-tuple-element.247), channel_id=1, source_target_pairs={{0,8},{1,9},{2,10},{3,11},{4,12},{5,13},{6,14},{7,15},{8,0},{9,1},... | collective-permute-start | bytes 1859336 | tf_op jit(solution)/shard_map/ppermute | solution.py:390
  313.0 20.3 %collective-permute-start.32 = (bf16[512,1152]{1,0:T(8,128)(2,1)S(1)}, bf16[512,1152]{1,0:T(8,128)(2,1)S(1)}, u32[]{:S(2)}, u32[]{:S(2)}) collective-permute-start(bf16[512,1152]{1,0:T(8,128)(2,1)S(1)} %slice.419), channel_id=1, source_target_pairs={{0,1},{1,0},{2,3},{3,2},{4,5},{5,4},{6,7},{7,6},{8,9},{9,8},{10,11... | collective-permute-start | bytes 3538952 | tf_op jit(solution)/shard_map/ppermute | solution.py:390
  320.6 12.9 %collective-permute-start.31 = (bf16[512,1152]{1,0:T(8,128)(2,1)S(1)}, bf16[512,1152]{1,0:T(8,128)(2,1)S(1)}, u32[]{:S(2)}, u32[]{:S(2)}) collective-permute-start(bf16[512,1152]{1,0:T(8,128)(2,1)S(1)} %slice.420), channel_id=1, source_target_pairs={{0,1},{1,0},{2,3},{3,2},{4,5},{5,4},{6,7},{7,6},{8,9},{9,8},{10,11... | collective-permute-start | bytes 3538952 | tf_op jit(solution)/shard_map/ppermute | solution.py:390
  321.2 21.4 %collective-permute-start.40 = (bf16[1,144,288]{2,1,0:T(8,128)(2,1)S(1)}, bf16[1,144,288]{2,1,0:T(8,128)(2,1)S(1)}, u32[]{:S(2)}, u32[]{:S(2)}) collective-permute-start(bf16[1,144,288]{2,1,0:T(8,128)(2,1)S(1)} %add_convert_fusion.26), channel_id=1, source_target_pairs={{0,16},{1,17},{2,18},{3,19},{4,20},{5,21},{6,22},{7,23},{8,24},{9,... | collective-permute-start | bytes 248840 | tf_op jit(solution)/shard_map/ppermute | solution.py:390
  331.1 16.2 %collective-permute-start.39 = (bf16[1,144,1076]{2,1,0:T(8,128)(2,1)}, bf16[1,144,1076]{2,1,0:T(8,128)(2,1)}, u32[]{:S(2)}, u32[]{:S(2)}) collective-permute-start(bf16[1,144,1076]{2,1,0:T(8,128)(2,1)} %add_convert_fusion.18), channel_id=1, source_target_pairs={{0,16},{1,17},{2,18},{3,19},{4,20},{5,21},{6,22},{7,23},{8,24},{9,... | collective-permute-start | bytes 929672 | tf_op jit(solution)/shard_map/ppermute | solution.py:390
  339.0 14.8 %collective-permute-start.38 = (bf16[4,144,864]{2,1,0:T(8,128)(2,1)}, bf16[4,144,864]{2,1,0:T(8,128)(2,1)S(1)}, u32[]{:S(2)}, u32[]{:S(2)}) collective-permute-start(bf16[4,144,864]{2,1,0:T(8,128)(2,1)} %get-tuple-element.245), channel_id=1, source_target_pairs={{0,4},{1,3},{2,6},{3,1},{4,0},{5,7},{6,2},{7,5},{8,12},{9,11},{10,... | collective-permute-start | bytes 2985992 | tf_op jit(solution)/shard_map/ppermute | solution.py:390
  354.1 12.6 %collective-permute-start.42 = (bf16[2,144,864]{2,1,0:T(8,128)(2,1)S(1)}, bf16[2,144,864]{2,1,0:T(8,128)(2,1)S(1)}, u32[]{:S(2)}, u32[]{:S(2)}) collective-permute-start(bf16[2,144,864]{2,1,0:T(8,128)(2,1)S(1)} %get-tuple-element.251), channel_id=1, source_target_pairs={{0,8},{1,9},{2,10},{3,11},{4,12},{5,13},{6,14},{7,15},{8,0},{9,1},... | collective-permute-start | bytes 1493000 | tf_op jit(solution)/shard_map/ppermute | solution.py:390
  (101 other events, 1108.4 us)
